TPU v7x, 32 devices: a whole 2x2x4 slice. The times are simulated.
32 devices in a mesh: groups: 2 (over x), expert: 16 (over z, y, core).
Axes of the slice: x: 2, y: 2, z: 4, core: 2. Of those that a mesh axis runs over, the one named last changes fastest.
Arguments:
- tokens: bfloat16 [2, 2048, 2048], P(None, ('groups', 'expert')), parts along dimension 1, may hold values from -6 to 6
- w_gate: bfloat16 [16, 2048, 768], P('expert'), may hold values from -0.125 to 0.125
- w_up: bfloat16 [16, 2048, 768], P('expert'), may hold values from -0.125 to 0.125
- w_down: bfloat16 [16, 768, 2048], P('expert'), may hold values from -0.21875 to 0.21875
- hot_gate: bfloat16 [2, 2048, 768], P(None, None, 'expert'), may hold values from -0.125 to 0.125
- hot_up: bfloat16 [2, 2048, 768], P(None, None, 'expert'), may hold values from -0.125 to 0.125
- hot_down: bfloat16 [2, 2048, 768], P(None, None, 'expert'), may hold values from -0.21875 to 0.21875
- cold_routes: int32 [2, 2048, 7], P(None, ('groups', 'expert')), parts along dimension 1, may hold values from 0 to 15, all different within a row; in each aligned block of 64 rows (0 to 63, 64 to 127, ..., all dimensions but the last counted through in order) at most 43 rows name the same one
- hot_pick: int32 [2, 2048], P(None, ('groups', 'expert')), parts along dimension 1, may hold values from 0 to 1, as said below
- gates: float32 [2, 2048, 8], P(None, ('groups', 'expert')), parts along dimension 1, may hold values from 0.1 to 1
Outputs:
- mixed: bfloat16 [2, 2048, 2048], P(None, ('groups', 'expert')), parts along dimension 1
There are 2 independent parts, one for each index of `groups`. A program takes and returns all parts, laid end to end along the dimension named above; an argument that names none is the same for every part. Nothing has to cross between parts.
Inputs may be any that keep to these rules, and one draw needn't show every extreme that they name: `hot_pick`: in each aligned block of 64 tokens of one micro-batch, each hot expert is picked by exactly 32 tokens. `cold_routes`: A token names 8 - 1 different cold experts; in each aligned block of 64 tokens of one micro-batch no cold expert is named more than 43 times.
All inputs are finite; a program needn't handle non-finite values.
Results may differ from a plain program's by a relative error of at most 0.0058.
Values may be sent and summed in bfloat16 or wider, within the bound.
No kernel may reach another device: no remote copies, remote signals or barrier semaphores. Data moves between devices by JAX's collectives and lax.ppermute only.
A program may use at most 128 MiB of HBM per device.

v0:
```python
import functools

import jax
import jax.numpy as jnp
from jax import lax
from jax.experimental import pallas as pl
from jax.experimental.pallas import tpu as pltpu
from jax.sharding import PartitionSpec as P

LANES = 128
PIECE = 32
SLOT = 8
HOT_GATE = 2 * PIECE
HOT_PICK = HOT_GATE + 3


def ring_tables(devices):
    chips = devices // 2
    ring = list(range(0, chips, 2)) + list(range(chips - 1, 0, -2))
    around = []
    for place in range(chips):
        following, preceding = ring[(place + 1) % chips], ring[place - 1]
        around.append((2 * ring[place], 2 * following))
        around.append((2 * ring[place] + 1, 2 * preceding + 1))
    across = [(device, device ^ 1) for device in range(devices)]
    return around, across


def tile_of(size, most):
    tile = most
    while size % tile:
        tile //= 2
    return tile


def silu(value):
    return value / (1.0 + jnp.exp(-value))


def work_body(me_ref, mine, shared, gate, up, down, hot_in, hot_out, y_mine, y_shared, rows, hidden, hot_hidden, *, hots):
    count, width = y_mine.shape
    units = gate.shape[1]
    rows[:count] = mine[:, :width]
    rows[count:] = shared[:, :width]
    facts = jnp.concatenate([mine[:, width:], shared[:, width:]], axis=0).astype(jnp.float32)
    lane = lax.broadcasted_iota(jnp.int32, facts.shape, 1)
    named = (facts == me_ref[0].astype(jnp.float32)) & (lane < 3 * SLOT)
    pieces = pltpu.roll(facts, LANES - PIECE, 1)
    cold_weight = jnp.sum(jnp.where(named, pieces, 0.0), axis=1, keepdims=True)
    is_hot = (lane >= HOT_GATE) & (lane < HOT_PICK)
    hot_weight = jnp.sum(jnp.where(is_hot, facts, 0.0), axis=1, keepdims=True)
    hot_pick = jnp.sum(jnp.where(lane == HOT_PICK, facts, 0.0), axis=1, keepdims=True)

    split = hot_in.shape[1] // 2
    both = jnp.dot(rows[...], hot_in[...], preferred_element_type=jnp.float32)
    value = silu(both[:, :split]) * both[:, split:]
    owner = lax.broadcasted_iota(jnp.int32, value.shape, 1) // (split // hots)
    hot_hidden[...] = jnp.where(owner.astype(jnp.float32) == hot_pick, value, 0.0).astype(jnp.bfloat16)

    tile = tile_of(units, 256)
    for start in range(0, units, tile):
        cut = slice(start, start + tile)
        a = jnp.dot(rows[...], gate[:, cut], preferred_element_type=jnp.float32)
        b = jnp.dot(rows[...], up[:, cut], preferred_element_type=jnp.float32)
        hidden[:, cut] = (silu(a) * b).astype(jnp.bfloat16)
    tile = tile_of(width, 512)
    for start in range(0, width, tile):
        cut = slice(start, start + tile)
        y = cold_weight * jnp.dot(hidden[...], down[:, cut], preferred_element_type=jnp.float32)
        y = y + hot_weight * jnp.dot(hot_hidden[...], hot_out[:, cut], preferred_element_type=jnp.float32)
        y_mine[:, cut] = y[:count].astype(y_mine.dtype)
        y_shared[:, cut] = y[count:].astype(y_shared.dtype)


def work(me, mine, shared, weights, hots):
    count = mine.shape[0]
    width, units = weights[0].shape
    hot_units = weights[4].shape[0]
    whole = pl.BlockSpec(memory_space=pltpu.VMEM)
    return pl.pallas_call(
        functools.partial(work_body, hots=hots),
        in_specs=[pl.BlockSpec(memory_space=pltpu.SMEM)] + [whole] * 7,
        out_specs=[whole] * 2,
        out_shape=[jax.ShapeDtypeStruct((count, width), jnp.bfloat16)] * 2,
        scratch_shapes=[
            pltpu.VMEM((2 * count, width), jnp.bfloat16),
            pltpu.VMEM((2 * count, units), jnp.bfloat16),
            pltpu.VMEM((2 * count, hot_units), jnp.bfloat16),
        ],
        compiler_params=pltpu.CompilerParams(vmem_limit_bytes=40 << 20),
        cost_estimate=pl.CostEstimate(
            flops=2 * 2 * count * width * 3 * (units + hot_units),
            bytes_accessed=2 * 4 * count * width,
            transcendentals=2 * count * units,
        ),
    )(me, mine, shared, *weights)


def facts_of(cold_routes, hot_pick, gates):
    high = lax.reduce_precision(gates, 8, 7)
    middle = lax.reduce_precision(gates - high, 8, 7)
    low = gates - high - middle
    pieces = [high, middle, low]
    lead = gates.shape[:-1]
    picks = cold_routes.astype(jnp.float32)
    gap = jnp.full(lead + (SLOT - picks.shape[-1],), -1.0, jnp.float32)
    hollow = jnp.zeros(lead + (SLOT - picks.shape[-1],), jnp.float32)
    columns = [picks, gap] * 3 + [jnp.zeros(lead + (PIECE - 3 * SLOT,), jnp.float32)]
    for piece in pieces:
        columns += [piece[..., 1:], hollow]
    columns += [jnp.zeros(lead + (PIECE - 3 * SLOT,), jnp.float32)]
    columns += [piece[..., :1] for piece in pieces] + [hot_pick[..., None].astype(jnp.float32)]
    columns += [jnp.zeros(lead + (LANES - HOT_PICK - 1,), jnp.float32)]
    return jnp.concatenate(columns, axis=-1).astype(jnp.bfloat16)


def shards(tokens, w_gate, w_up, w_down, hot_gate, hot_up, hot_down, cold_routes, hot_pick, gates):
    devices = lax.axis_size("expert")
    micros, held, width = tokens.shape
    hots = hot_gate.shape[0]
    chips = devices // 2
    around, across = ring_tables(devices)
    me = lax.axis_index("expert").astype(jnp.int32).reshape(1)

    def swap(x):
        return lax.ppermute(x, "expert", across)

    def onward(x):
        return lax.ppermute(x, "expert", around)

    rows = jnp.concatenate([tokens, facts_of(cold_routes, hot_pick, gates)], axis=-1)
    rows = rows.reshape(micros * held, rows.shape[-1])
    hot_in = jnp.concatenate([w[h] for w in (hot_gate, hot_up) for h in range(hots)], axis=1)
    hot_out = jnp.concatenate([hot_down[h].T for h in range(hots)], axis=0)
    weights = (w_gate[0], w_up[0], w_down[0], hot_in, hot_out)

    own = work(me, rows, swap(rows), weights, hots)
    coming = None
    mine = rows
    for step in range(1, chips):
        mine = onward(mine)
        kept, given = work(me, mine, swap(mine), weights, hots)
        total = kept.astype(jnp.float32) + swap(given).astype(jnp.float32)
        if coming is not None:
            total = total + coming.astype(jnp.float32)
        coming = onward(total.astype(jnp.bfloat16))
    total = own[0].astype(jnp.float32) + swap(own[1]).astype(jnp.float32) + coming.astype(jnp.float32)
    return total.astype(jnp.bfloat16).reshape(micros, held, width)


def solution(mesh):
    in_specs = (
        P(None, ("groups", "expert"), None),
        P("expert", None, None),
        P("expert", None, None),
        P("expert", None, None),
        P(None, None, "expert"),
        P(None, None, "expert"),
        P(None, None, "expert"),
        P(None, ("groups", "expert"), None),
        P(None, ("groups", "expert")),
        P(None, ("groups", "expert"), None),
    )
    out_specs = P(None, ("groups", "expert"), None)
    return jax.shard_map(shards, mesh=mesh, in_specs=in_specs, out_specs=out_specs, check_vma=False)
```

profile of v0, /device:TPU:0, one launch (start us, length us, event | category | flops | bytes accessed | tf_op | source)
XLA Modules:
  0.0 117.9 jit_solution(9402308983223763945)
XLA Ops:
  4.6 3.1 %collective-permute-start.2 = (bf16[128,2176]{1,0:T(8,128)(2,1)S(1)}, bf16[128,2176]{1,0:T(8,128)(2,1)}, u32[]{:S(2)}, u32[]{:S(2)}) collective-permute-start(bf16[128,2176]{1,0:T(8,128)(2,1)S(1)} %bitcast.44), channel_id=1, source_target_pairs={{0,4},{1,3},{4,8},{5,1},{8,12},{9,5},{12,14},{13,9},{14,10},{15,13... | collective-permute-start | bytes 1671176 | tf_op jit(solution)/shard_map/ppermute | solution.py:129
  8.5 6.8 %collective-permute-done.2.mine = bf16[128,2176]{1,0:T(8,128)(2,1)} collective-permute-done((bf16[128,2176]{1,0:T(8,128)(2,1)S(1)}, bf16[128,2176]{1,0:T(8,128)(2,1)}, u32[]{:S(2)}, u32[]{:S(2)}) %collective-permute-start.2) | collective-permute-done | bytes 557088 | tf_op jit(solution)/shard_map/ppermute | solution.py:129
  23.2 2.4 %pad_maximum_fusion.hot_in = bf16[2048,192]{1,0:T(8,128)(2,1)S(1)} fusion(bf16[2048,48]{1,0:T(8,128)(2,1)} %bitcast.49, bf16[2048,48]{1,0:T(8,128)(2,1)} %bitcast.48, bf16[2048,48]{1,0:T(8,128)(2,1)} %bitcast.50, bf16[2048,48]{1,0:T(8,128)(2,1)} %bitcast.47), kind=kLoop, calls=%fused_computation | loop fusion | flops 3145728 | bytes 1572864 | tf_op jit(solution)/shard_map/concatenate | solution.py:133
  25.7 2.1 %collective-permute-start.3 = (bf16[128,2176]{1,0:T(8,128)(2,1)}, bf16[128,2176]{1,0:T(8,128)(2,1)S(1)}, u32[]{:S(2)}, u32[]{:S(2)}) collective-permute-start(bf16[128,2176]{1,0:T(8,128)(2,1)} %collective-permute-done.2.mine), channel_id=1, source_target_pairs={{0,4},{1,3},{4,8},{5,1},{8,12},{9,5},{12,14},{13,9},{14,10},{15,13... | collective-permute-start | bytes 1671176 | tf_op jit(solution)/shard_map/ppermute | solution.py:129
  29.7 4.9 %shard_map.107 = (bf16[128,2048]{1,0:T(8,128)(2,1)S(1)}, bf16[128,2048]{1,0:T(8,128)(2,1)S(1)}) custom-call(s32[1]{0:T(128)} %bitcast.me_ref, bf16[128,2176]{1,0:T(8,128)(2,1)} %collective-permute-done.2.mine, bf16[128,2176]{1,0:T(8,128)(2,1)} %collective-permute-done.21.shared, bf16[2048,768]{1,0:T(8,128)(2,1)S(1)} %bitcast.20, ...), custom_call_target="tpu_custom_call" | custom-call | flops 2717908992 | bytes 2097152 | tf_op jit(solution)/shard_map/pallas_call | solution.py:80
  35.5 2.1 %collective-permute-start.4 = (bf16[128,2176]{1,0:T(8,128)(2,1)S(1)}, bf16[128,2176]{1,0:T(8,128)(2,1)S(1)}, u32[]{:S(2)}, u32[]{:S(2)}) collective-permute-start(bf16[128,2176]{1,0:T(8,128)(2,1)S(1)} %collective-permute-done.3.mine), channel_id=1, source_target_pairs={{0,4},{1,3},{4,8},{5,1},{8,12},{9,5},{12,14},{13,9},{14,10},{15,13... | collective-permute-start | bytes 1671176 | tf_op jit(solution)/shard_map/ppermute | solution.py:129
  39.3 3.7 %shard_map.106 = (bf16[128,2048]{1,0:T(8,128)(2,1)S(1)}, bf16[128,2048]{1,0:T(8,128)(2,1)S(1)}) custom-call(s32[1]{0:T(128)} %bitcast.me_ref, bf16[128,2176]{1,0:T(8,128)(2,1)S(1)} %collective-permute-done.3.mine, bf16[128,2176]{1,0:T(8,128)(2,1)S(1)} %collective-permute-done.19.shared, bf16[2048,768]{1,0:T(8,128)(2,1)S(1)} %bitcast.21, ...), custom_call_target="tpu_custom_call" | custom-call | flops 2717908992 | bytes 2097152 | tf_op jit(solution)/shard_map/pallas_call | solution.py:80
  47.1 3.5 %collective-permute-done.23 = bf16[128,2048]{1,0:T(8,128)(2,1)S(1)} collective-permute-done((bf16[128,2048]{1,0:T(8,128)(2,1)S(1)}, bf16[128,2048]{1,0:T(8,128)(2,1)S(1)}, u32[]{:S(2)}, u32[]{:S(2)}) %collective-permute-start.23) | collective-permute-done | bytes 524320 | tf_op jit(solution)/shard_map/ppermute | solution.py:129
  50.9 2.3 %collective-permute-start.24 = (bf16[128,2048]{1,0:T(8,128)(2,1)S(1)}, bf16[128,2048]{1,0:T(8,128)(2,1)S(1)}, u32[]{:S(2)}, u32[]{:S(2)}) collective-permute-start(bf16[128,2048]{1,0:T(8,128)(2,1)S(1)} %add_convert_fusion.6), channel_id=1, source_target_pairs={{0,4},{1,3},{4,8},{5,1},{8,12},{9,5},{12,14},{13,9},{14,10},{15,13... | collective-permute-start | bytes 1572872 | tf_op jit(solution)/shard_map/ppermute | solution.py:129
  53.2 3.7 %shard_map.105 = (bf16[128,2048]{1,0:T(8,128)(2,1)S(1)}, bf16[128,2048]{1,0:T(8,128)(2,1)S(1)}) custom-call(s32[1]{0:T(128)} %bitcast.me_ref, bf16[128,2176]{1,0:T(8,128)(2,1)S(1)} %collective-permute-done.4.mine, bf16[128,2176]{1,0:T(8,128)(2,1)S(1)} %collective-permute-done.17.shared, bf16[2048,768]{1,0:T(8,128)(2,1)S(1)} %bitcast.22, ...), custom_call_target="tpu_custom_call" | custom-call | flops 2717908992 | bytes 2097152 | tf_op jit(solution)/shard_map/pallas_call | solution.py:80
  59.0 3.2 %collective-permute-done.24 = bf16[128,2048]{1,0:T(8,128)(2,1)S(1)} collective-permute-done((bf16[128,2048]{1,0:T(8,128)(2,1)S(1)}, bf16[128,2048]{1,0:T(8,128)(2,1)S(1)}, u32[]{:S(2)}, u32[]{:S(2)}) %collective-permute-start.24) | collective-permute-done | bytes 524320 | tf_op jit(solution)/shard_map/ppermute | solution.py:129
  62.4 2.1 %collective-permute-start.25 = (bf16[128,2048]{1,0:T(8,128)(2,1)S(1)}, bf16[128,2048]{1,0:T(8,128)(2,1)S(1)}, u32[]{:S(2)}, u32[]{:S(2)}) collective-permute-start(bf16[128,2048]{1,0:T(8,128)(2,1)S(1)} %add_convert_fusion.5), channel_id=1, source_target_pairs={{0,4},{1,3},{4,8},{5,1},{8,12},{9,5},{12,14},{13,9},{14,10},{15,13... | collective-permute-start | bytes 1572872 | tf_op jit(solution)/shard_map/ppermute | solution.py:129
  64.6 3.7 %shard_map.104 = (bf16[128,2048]{1,0:T(8,128)(2,1)S(1)}, bf16[128,2048]{1,0:T(8,128)(2,1)S(1)}) custom-call(s32[1]{0:T(128)} %bitcast.me_ref, bf16[128,2176]{1,0:T(8,128)(2,1)S(1)} %collective-permute-done.5.mine, bf16[128,2176]{1,0:T(8,128)(2,1)S(1)} %collective-permute-done.15.shared, bf16[2048,768]{1,0:T(8,128)(2,1)S(1)} %bitcast.23, ...), custom_call_target="tpu_custom_call" | custom-call | flops 2717908992 | bytes 2097152 | tf_op jit(solution)/shard_map/pallas_call | solution.py:80
  70.4 3.4 %collective-permute-done.25 = bf16[128,2048]{1,0:T(8,128)(2,1)S(1)} collective-permute-done((bf16[128,2048]{1,0:T(8,128)(2,1)S(1)}, bf16[128,2048]{1,0:T(8,128)(2,1)S(1)}, u32[]{:S(2)}, u32[]{:S(2)}) %collective-permute-start.25) | collective-permute-done | bytes 524320 | tf_op jit(solution)/shard_map/ppermute | solution.py:129
  74.0 2.1 %collective-permute-start.26 = (bf16[128,2048]{1,0:T(8,128)(2,1)S(1)}, bf16[128,2048]{1,0:T(8,128)(2,1)S(1)}, u32[]{:S(2)}, u32[]{:S(2)}) collective-permute-start(bf16[128,2048]{1,0:T(8,128)(2,1)S(1)} %add_convert_fusion.4), channel_id=1, source_target_pairs={{0,4},{1,3},{4,8},{5,1},{8,12},{9,5},{12,14},{13,9},{14,10},{15,13... | collective-permute-start | bytes 1572872 | tf_op jit(solution)/shard_map/ppermute | solution.py:129
  76.2 3.7 %shard_map.103 = (bf16[128,2048]{1,0:T(8,128)(2,1)S(1)}, bf16[128,2048]{1,0:T(8,128)(2,1)S(1)}) custom-call(s32[1]{0:T(128)} %bitcast.me_ref, bf16[128,2176]{1,0:T(8,128)(2,1)S(1)} %collective-permute-done.6.mine, bf16[128,2176]{1,0:T(8,128)(2,1)S(1)} %collective-permute-done.13.shared, bf16[2048,768]{1,0:T(8,128)(2,1)S(1)} %bitcast.24, ...), custom_call_target="tpu_custom_call" | custom-call | flops 2717908992 | bytes 2097152 | tf_op jit(solution)/shard_map/pallas_call | solution.py:80
  82.0 3.4 %collective-permute-done.26 = bf16[128,2048]{1,0:T(8,128)(2,1)S(1)} collective-permute-done((bf16[128,2048]{1,0:T(8,128)(2,1)S(1)}, bf16[128,2048]{1,0:T(8,128)(2,1)S(1)}, u32[]{:S(2)}, u32[]{:S(2)}) %collective-permute-start.26) | collective-permute-done | bytes 524320 | tf_op jit(solution)/shard_map/ppermute | solution.py:129
  85.6 2.3 %collective-permute-start.27 = (bf16[128,2048]{1,0:T(8,128)(2,1)S(1)}, bf16[128,2048]{1,0:T(8,128)(2,1)S(1)}, u32[]{:S(2)}, u32[]{:S(2)}) collective-permute-start(bf16[128,2048]{1,0:T(8,128)(2,1)S(1)} %add_convert_fusion.3), channel_id=1, source_target_pairs={{0,4},{1,3},{4,8},{5,1},{8,12},{9,5},{12,14},{13,9},{14,10},{15,13... | collective-permute-start | bytes 1572872 | tf_op jit(solution)/shard_map/ppermute | solution.py:129
  88.0 3.7 %shard_map.102 = (bf16[128,2048]{1,0:T(8,128)(2,1)S(1)}, bf16[128,2048]{1,0:T(8,128)(2,1)S(1)}) custom-call(s32[1]{0:T(128)} %bitcast.me_ref, bf16[128,2176]{1,0:T(8,128)(2,1)S(1)} %collective-permute-done.7.mine, bf16[128,2176]{1,0:T(8,128)(2,1)S(1)} %collective-permute-done.11.shared, bf16[2048,768]{1,0:T(8,128)(2,1)S(1)} %bitcast.25, ...), custom_call_target="tpu_custom_call" | custom-call | flops 2717908992 | bytes 2097152 | tf_op jit(solution)/shard_map/pallas_call | solution.py:80
  92.3 4.6 %collective-permute-done.27 = bf16[128,2048]{1,0:T(8,128)(2,1)S(1)} collective-permute-done((bf16[128,2048]{1,0:T(8,128)(2,1)S(1)}, bf16[128,2048]{1,0:T(8,128)(2,1)S(1)}, u32[]{:S(2)}, u32[]{:S(2)}) %collective-permute-start.27) | collective-permute-done | bytes 524320 | tf_op jit(solution)/shard_map/ppermute | solution.py:129
  97.2 2.1 %collective-permute-start.28 = (bf16[128,2048]{1,0:T(8,128)(2,1)S(1)}, bf16[128,2048]{1,0:T(8,128)(2,1)S(1)}, u32[]{:S(2)}, u32[]{:S(2)}) collective-permute-start(bf16[128,2048]{1,0:T(8,128)(2,1)S(1)} %add_convert_fusion.2), channel_id=1, source_target_pairs={{0,4},{1,3},{4,8},{5,1},{8,12},{9,5},{12,14},{13,9},{14,10},{15,13... | collective-permute-start | bytes 1572872 | tf_op jit(solution)/shard_map/ppermute | solution.py:129
  99.3 3.7 %shard_map.101 = (bf16[128,2048]{1,0:T(8,128)(2,1)S(1)}, bf16[128,2048]{1,0:T(8,128)(2,1)S(1)}) custom-call(s32[1]{0:T(128)} %bitcast.me_ref, bf16[128,2176]{1,0:T(8,128)(2,1)S(1)} %collective-permute-done.8.mine, bf16[128,2176]{1,0:T(8,128)(2,1)S(1)} %collective-permute-done.9.shared, bf16[2048,768]{1,0:T(8,128)(2,1)S(1)} %bitcast.26, ...), custom_call_target="tpu_custom_call" | custom-call | flops 2717908992 | bytes 2097152 | tf_op jit(solution)/shard_map/pallas_call | solution.py:80
  103.1 3.7 %shard_map.100 = (bf16[128,2048]{1,0:T(8,128)(2,1)S(1)}, bf16[128,2048]{1,0:T(8,128)(2,1)S(1)}) custom-call(s32[1]{0:T(128)} %bitcast.me_ref, bf16[128,2176]{1,0:T(8,128)(2,1)S(1)} %bitcast.46, bf16[128,2176]{1,0:T(8,128)(2,1)S(1)} %collective-permute-done.shared, bf16[2048,768]{1,0:T(8,128)(2,1)S(1)} %bitcast.27, bf16[2048,768]{1,0:T(8,128)(2,1)S(1)} %bitcast.35, ...), custom_call_target="tpu_custom_call" | custom-call | flops 2717908992 | bytes 2097152 | tf_op jit(solution)/shard_map/pallas_call | solution.py:80
  109.2 7.6 %collective-permute-done.29 = bf16[128,2048]{1,0:T(8,128)(2,1)S(1)} collective-permute-done((bf16[128,2048]{1,0:T(8,128)(2,1)S(1)}, bf16[128,2048]{1,0:T(8,128)(2,1)S(1)}, u32[]{:S(2)}, u32[]{:S(2)}) %collective-permute-start.29) | collective-permute-done | bytes 524320 | tf_op jit(solution)/shard_map/ppermute | solution.py:129
  (99 shorter events, 33.7 us)
Async XLA Ops:
  4.6 10.6 %collective-permute-start.2 = (bf16[128,2176]{1,0:T(8,128)(2,1)S(1)}, bf16[128,2176]{1,0:T(8,128)(2,1)}, u32[]{:S(2)}, u32[]{:S(2)}) collective-permute-start(bf16[128,2176]{1,0:T(8,128)(2,1)S(1)} %bitcast.44), channel_id=1, source_target_pairs={{0,4},{1,3},{4,8},{5,1},{8,12},{9,5},{12,14},{13,9},{14,10},{15,13... | collective-permute-start | bytes 1671176 | tf_op jit(solution)/shard_map/ppermute | solution.py:129
  15.3 12.5 %collective-permute-start.21 = (bf16[128,2176]{1,0:T(8,128)(2,1)}, bf16[128,2176]{1,0:T(8,128)(2,1)}, u32[]{:S(2)}, u32[]{:S(2)}) collective-permute-start(bf16[128,2176]{1,0:T(8,128)(2,1)} %collective-permute-done.2.mine), channel_id=1, source_target_pairs={{0,1},{1,0},{2,3},{3,2},{4,5},{5,4},{6,7},{7,6},{8,9},{9,8},{10,11... | collective-permute-start | bytes 1671176 | tf_op jit(solution)/shard_map/ppermute | solution.py:126
  25.7 9.8 %collective-permute-start.3 = (bf16[128,2176]{1,0:T(8,128)(2,1)}, bf16[128,2176]{1,0:T(8,128)(2,1)S(1)}, u32[]{:S(2)}, u32[]{:S(2)}) collective-permute-start(bf16[128,2176]{1,0:T(8,128)(2,1)} %collective-permute-done.2.mine), channel_id=1, source_target_pairs={{0,4},{1,3},{4,8},{5,1},{8,12},{9,5},{12,14},{13,9},{14,10},{15,13... | collective-permute-start | bytes 1671176 | tf_op jit(solution)/shard_map/ppermute | solution.py:129
  35.5 9.5 %collective-permute-start.4 = (bf16[128,2176]{1,0:T(8,128)(2,1)S(1)}, bf16[128,2176]{1,0:T(8,128)(2,1)S(1)}, u32[]{:S(2)}, u32[]{:S(2)}) collective-permute-start(bf16[128,2176]{1,0:T(8,128)(2,1)S(1)} %collective-permute-done.3.mine), channel_id=1, source_target_pairs={{0,4},{1,3},{4,8},{5,1},{8,12},{9,5},{12,14},{13,9},{14,10},{15,13... | collective-permute-start | bytes 1671176 | tf_op jit(solution)/shard_map/ppermute | solution.py:129
  37.7 12.9 %collective-permute-start.23 = (bf16[128,2048]{1,0:T(8,128)(2,1)S(1)}, bf16[128,2048]{1,0:T(8,128)(2,1)S(1)}, u32[]{:S(2)}, u32[]{:S(2)}) collective-permute-start(bf16[128,2048]{1,0:T(8,128)(2,1)S(1)} %add_convert_fusion.7), channel_id=1, source_target_pairs={{0,4},{1,3},{4,8},{5,1},{8,12},{9,5},{12,14},{13,9},{14,10},{15,13... | collective-permute-start | bytes 1572872 | tf_op jit(solution)/shard_map/ppermute | solution.py:129
  43.0 7.6 %collective-permute-start.20 = (bf16[128,2048]{1,0:T(8,128)(2,1)S(1)}, bf16[128,2048]{1,0:T(8,128)(2,1)S(1)}, u32[]{:S(2)}, u32[]{:S(2)}) collective-permute-start(bf16[128,2048]{1,0:T(8,128)(2,1)S(1)} %get-tuple-element.34), channel_id=1, source_target_pairs={{0,1},{1,0},{2,3},{3,2},{4,5},{5,4},{6,7},{7,6},{8,9},{9,8},{10,11... | collective-permute-start | bytes 1572872 | tf_op jit(solution)/shard_map/ppermute | solution.py:126
  45.0 8.2 %collective-permute-start.17 = (bf16[128,2176]{1,0:T(8,128)(2,1)S(1)}, bf16[128,2176]{1,0:T(8,128)(2,1)S(1)}, u32[]{:S(2)}, u32[]{:S(2)}) collective-permute-start(bf16[128,2176]{1,0:T(8,128)(2,1)S(1)} %collective-permute-done.4.mine), channel_id=1, source_target_pairs={{0,1},{1,0},{2,3},{3,2},{4,5},{5,4},{6,7},{7,6},{8,9},{9,8},{10,11... | collective-permute-start | bytes 1671176 | tf_op jit(solution)/shard_map/ppermute | solution.py:126
  45.0 11.9 %collective-permute-start.5 = (bf16[128,2176]{1,0:T(8,128)(2,1)S(1)}, bf16[128,2176]{1,0:T(8,128)(2,1)S(1)}, u32[]{:S(2)}, u32[]{:S(2)}) collective-permute-start(bf16[128,2176]{1,0:T(8,128)(2,1)S(1)} %collective-permute-done.4.mine), channel_id=1, source_target_pairs={{0,4},{1,3},{4,8},{5,1},{8,12},{9,5},{12,14},{13,9},{14,10},{15,13... | collective-permute-start | bytes 1671176 | tf_op jit(solution)/shard_map/ppermute | solution.py:129
  50.9 11.3 %collective-permute-start.24 = (bf16[128,2048]{1,0:T(8,128)(2,1)S(1)}, bf16[128,2048]{1,0:T(8,128)(2,1)S(1)}, u32[]{:S(2)}, u32[]{:S(2)}) collective-permute-start(bf16[128,2048]{1,0:T(8,128)(2,1)S(1)} %add_convert_fusion.6), channel_id=1, source_target_pairs={{0,4},{1,3},{4,8},{5,1},{8,12},{9,5},{12,14},{13,9},{14,10},{15,13... | collective-permute-start | bytes 1572872 | tf_op jit(solution)/shard_map/ppermute | solution.py:129
  56.9 7.6 %collective-permute-start.15 = (bf16[128,2176]{1,0:T(8,128)(2,1)S(1)}, bf16[128,2176]{1,0:T(8,128)(2,1)S(1)}, u32[]{:S(2)}, u32[]{:S(2)}) collective-permute-start(bf16[128,2176]{1,0:T(8,128)(2,1)S(1)} %collective-permute-done.5.mine), channel_id=1, source_target_pairs={{0,1},{1,0},{2,3},{3,2},{4,5},{5,4},{6,7},{7,6},{8,9},{9,8},{10,11... | collective-permute-start | bytes 1671176 | tf_op jit(solution)/shard_map/ppermute | solution.py:126
  57.4 10.9 %collective-permute-start.6 = (bf16[128,2176]{1,0:T(8,128)(2,1)S(1)}, bf16[128,2176]{1,0:T(8,128)(2,1)S(1)}, u32[]{:S(2)}, u32[]{:S(2)}) collective-permute-start(bf16[128,2176]{1,0:T(8,128)(2,1)S(1)} %collective-permute-done.5.mine), channel_id=1, source_target_pairs={{0,4},{1,3},{4,8},{5,1},{8,12},{9,5},{12,14},{13,9},{14,10},{15,13... | collective-permute-start | bytes 1671176 | tf_op jit(solution)/shard_map/ppermute | solution.py:129
  62.4 11.3 %collective-permute-start.25 = (bf16[128,2048]{1,0:T(8,128)(2,1)S(1)}, bf16[128,2048]{1,0:T(8,128)(2,1)S(1)}, u32[]{:S(2)}, u32[]{:S(2)}) collective-permute-start(bf16[128,2048]{1,0:T(8,128)(2,1)S(1)} %add_convert_fusion.5), channel_id=1, source_target_pairs={{0,4},{1,3},{4,8},{5,1},{8,12},{9,5},{12,14},{13,9},{14,10},{15,13... | collective-permute-start | bytes 1572872 | tf_op jit(solution)/shard_map/ppermute | solution.py:129
  68.3 5.5 %collective-permute-start.16 = (bf16[128,2048]{1,0:T(8,128)(2,1)S(1)}, bf16[128,2048]{1,0:T(8,128)(2,1)S(1)}, u32[]{:S(2)}, u32[]{:S(2)}) collective-permute-start(bf16[128,2048]{1,0:T(8,128)(2,1)S(1)} %get-tuple-element.30), channel_id=1, source_target_pairs={{0,1},{1,0},{2,3},{3,2},{4,5},{5,4},{6,7},{7,6},{8,9},{9,8},{10,11... | collective-permute-start | bytes 1572872 | tf_op jit(solution)/shard_map/ppermute | solution.py:126
  68.4 7.8 %collective-permute-start.13 = (bf16[128,2176]{1,0:T(8,128)(2,1)S(1)}, bf16[128,2176]{1,0:T(8,128)(2,1)S(1)}, u32[]{:S(2)}, u32[]{:S(2)}) collective-permute-start(bf16[128,2176]{1,0:T(8,128)(2,1)S(1)} %collective-permute-done.6.mine), channel_id=1, source_target_pairs={{0,1},{1,0},{2,3},{3,2},{4,5},{5,4},{6,7},{7,6},{8,9},{9,8},{10,11... | collective-permute-start | bytes 1671176 | tf_op jit(solution)/shard_map/ppermute | solution.py:126
  68.8 11.1 %collective-permute-start.7 = (bf16[128,2176]{1,0:T(8,128)(2,1)S(1)}, bf16[128,2176]{1,0:T(8,128)(2,1)S(1)}, u32[]{:S(2)}, u32[]{:S(2)}) collective-permute-start(bf16[128,2176]{1,0:T(8,128)(2,1)S(1)} %collective-permute-done.6.mine), channel_id=1, source_target_pairs={{0,4},{1,3},{4,8},{5,1},{8,12},{9,5},{12,14},{13,9},{14,10},{15,13... | collective-permute-start | bytes 1671176 | tf_op jit(solution)/shard_map/ppermute | solution.py:129
  74.0 11.3 %collective-permute-start.26 = (bf16[128,2048]{1,0:T(8,128)(2,1)S(1)}, bf16[128,2048]{1,0:T(8,128)(2,1)S(1)}, u32[]{:S(2)}, u32[]{:S(2)}) collective-permute-start(bf16[128,2048]{1,0:T(8,128)(2,1)S(1)} %add_convert_fusion.4), channel_id=1, source_target_pairs={{0,4},{1,3},{4,8},{5,1},{8,12},{9,5},{12,14},{13,9},{14,10},{15,13... | collective-permute-start | bytes 1572872 | tf_op jit(solution)/shard_map/ppermute | solution.py:129
  79.9 5.5 %collective-permute-start.14 = (bf16[128,2048]{1,0:T(8,128)(2,1)S(1)}, bf16[128,2048]{1,0:T(8,128)(2,1)S(1)}, u32[]{:S(2)}, u32[]{:S(2)}) collective-permute-start(bf16[128,2048]{1,0:T(8,128)(2,1)S(1)} %get-tuple-element.28), channel_id=1, source_target_pairs={{0,1},{1,0},{2,3},{3,2},{4,5},{5,4},{6,7},{7,6},{8,9},{9,8},{10,11... | collective-permute-start | bytes 1572872 | tf_op jit(solution)/shard_map/ppermute | solution.py:126
  79.9 8.0 %collective-permute-start.11 = (bf16[128,2176]{1,0:T(8,128)(2,1)S(1)}, bf16[128,2176]{1,0:T(8,128)(2,1)S(1)}, u32[]{:S(2)}, u32[]{:S(2)}) collective-permute-start(bf16[128,2176]{1,0:T(8,128)(2,1)S(1)} %collective-permute-done.7.mine), channel_id=1, source_target_pairs={{0,1},{1,0},{2,3},{3,2},{4,5},{5,4},{6,7},{7,6},{8,9},{9,8},{10,11... | collective-permute-start | bytes 1671176 | tf_op jit(solution)/shard_map/ppermute | solution.py:126
  80.4 11.3 %collective-permute-start.8 = (bf16[128,2176]{1,0:T(8,128)(2,1)S(1)}, bf16[128,2176]{1,0:T(8,128)(2,1)S(1)}, u32[]{:S(2)}, u32[]{:S(2)}) collective-permute-start(bf16[128,2176]{1,0:T(8,128)(2,1)S(1)} %collective-permute-done.7.mine), channel_id=1, source_target_pairs={{0,4},{1,3},{4,8},{5,1},{8,12},{9,5},{12,14},{13,9},{14,10},{15,13... | collective-permute-start | bytes 1671176 | tf_op jit(solution)/shard_map/ppermute | solution.py:129
  85.6 11.3 %collective-permute-start.27 = (bf16[128,2048]{1,0:T(8,128)(2,1)S(1)}, bf16[128,2048]{1,0:T(8,128)(2,1)S(1)}, u32[]{:S(2)}, u32[]{:S(2)}) collective-permute-start(bf16[128,2048]{1,0:T(8,128)(2,1)S(1)} %add_convert_fusion.3), channel_id=1, source_target_pairs={{0,4},{1,3},{4,8},{5,1},{8,12},{9,5},{12,14},{13,9},{14,10},{15,13... | collective-permute-start | bytes 1572872 | tf_op jit(solution)/shard_map/ppermute | solution.py:129
  91.8 7.6 %collective-permute-start.9 = (bf16[128,2176]{1,0:T(8,128)(2,1)S(1)}, bf16[128,2176]{1,0:T(8,128)(2,1)S(1)}, u32[]{:S(2)}, u32[]{:S(2)}) collective-permute-start(bf16[128,2176]{1,0:T(8,128)(2,1)S(1)} %collective-permute-done.8.mine), channel_id=1, source_target_pairs={{0,1},{1,0},{2,3},{3,2},{4,5},{5,4},{6,7},{7,6},{8,9},{9,8},{10,11... | collective-permute-start | bytes 1671176 | tf_op jit(solution)/shard_map/ppermute | solution.py:126
  92.3 10.9 %collective-permute-start = (bf16[128,2176]{1,0:T(8,128)(2,1)S(1)}, bf16[128,2176]{1,0:T(8,128)(2,1)S(1)}, u32[]{:S(2)}, u32[]{:S(2)}) collective-permute-start(bf16[128,2176]{1,0:T(8,128)(2,1)S(1)} %bitcast.45), channel_id=1, source_target_pairs={{0,1},{1,0},{2,3},{3,2},{4,5},{5,4},{6,7},{7,6},{8,9},{9,8},{10,11... | collective-permute-start | bytes 1671176 | tf_op jit(solution)/shard_map/ppermute | solution.py:126
  97.2 10.2 %collective-permute-start.28 = (bf16[128,2048]{1,0:T(8,128)(2,1)S(1)}, bf16[128,2048]{1,0:T(8,128)(2,1)S(1)}, u32[]{:S(2)}, u32[]{:S(2)}) collective-permute-start(bf16[128,2048]{1,0:T(8,128)(2,1)S(1)} %add_convert_fusion.2), channel_id=1, source_target_pairs={{0,4},{1,3},{4,8},{5,1},{8,12},{9,5},{12,14},{13,9},{14,10},{15,13... | collective-permute-start | bytes 1572872 | tf_op jit(solution)/shard_map/ppermute | solution.py:129
  107.6 9.2 %collective-permute-start.29 = (bf16[128,2048]{1,0:T(8,128)(2,1)S(1)}, bf16[128,2048]{1,0:T(8,128)(2,1)S(1)}, u32[]{:S(2)}, u32[]{:S(2)}) collective-permute-start(bf16[128,2048]{1,0:T(8,128)(2,1)S(1)} %add_convert_fusion.1), channel_id=1, source_target_pairs={{0,4},{1,3},{4,8},{5,1},{8,12},{9,5},{12,14},{13,9},{14,10},{15,13... | collective-permute-start | bytes 1572872 | tf_op jit(solution)/shard_map/ppermute | solution.py:129
  (14 other events, 92.4 us)
where the time goes:
time: 118 us
  waiting for transfers between devices  35 us (30%)
  starting transfers between devices  31.7 us (27%)
  Pallas kernels  30.7 us (26%)
  local copies, waits for them, and re-layouts  11.8 us (10%)
  other arithmetic  8.42 us (7%)
    ppermute x14, waiting for transfers between devices, onward(): return lax.ppermute(x, 'expert', around)  34.9 us
    pallas_call x8, Pallas kernels, work(): pl.pallas_call(functools.partial(work_body, hots=hots), in_specs=[pl.Bloc...  30.7 us
    ppermute x14, starting transfers between devices, onward(): return lax.ppermute(x, 'expert', around)  28.4 us
    unnamed x20, local copies, waits for them, and re-layouts  7.88 us
    ppermute x16, starting transfers between devices, swap(): return lax.ppermute(x, 'expert', across)  3.26 us
    concatenate x1, other arithmetic, shards(): jnp.concatenate([w[h] for w in (hot_gate, hot_up) for h in range(hots)],...  2.43 us
  transfers between devices with their start and end apart: 30, of which 9 were waited for; matrix products, arithmetic and copies ran while one was open for 11% of the time, Pallas kernels for 26%

commit v1 on v0

v1 whole, which is shorter than its diff:
```python
import functools

import jax
import jax.numpy as jnp
from jax import lax
from jax.experimental import pallas as pl
from jax.experimental.pallas import tpu as pltpu
from jax.sharding import PartitionSpec as P

LANES = 128
PIECE = 32
SLOT = 8
HOT_GATE = 2 * PIECE
HOT_PICK = HOT_GATE + 3
FIRST_PARTS = 1
MERGE_AT = 3
OWN_AT = 1
LAST_PARTS = 1
LAST_STEPS = 2
ORDERED = True


def ring_tables(devices):
    chips = devices // 2
    ring = list(range(0, chips, 2)) + list(range(chips - 1, 0, -2))
    around = []
    for place in range(chips):
        following, preceding = ring[(place + 1) % chips], ring[place - 1]
        around.append((2 * ring[place], 2 * following))
        around.append((2 * ring[place] + 1, 2 * preceding + 1))
    across = [(device, device ^ 1) for device in range(devices)]
    return around, across


def tile_of(size, most):
    tile = most
    while size % tile:
        tile //= 2
    return tile


def silu(value):
    return value / (1.0 + jnp.exp(-value))


def rows_body(tokens, gates, routes, pick, *refs, micros, parts):
    outs, (gates_in, routes_in, pick_in, columns, done) = refs[:parts], refs[parts:]
    held, width = tokens.shape[1:]
    picks = routes.shape[0]
    share = micros // parts
    copies = [
        pltpu.make_async_copy(source, target, done.at[number])
        for number, (source, target) in enumerate(((gates, gates_in), (routes, routes_in), (pick, pick_in)))
    ]
    places = []
    for micro in range(micros):
        places.append((outs[micro // share], pl.ds(micro % share * held, held)))
        out, place = places[-1]
        copies.append(pltpu.make_async_copy(tokens.at[micro], out.at[place, pl.ds(0, width)], done.at[3 + micro]))
    for copy in copies:
        copy.start()
    for copy in copies[:3]:
        copy.wait()
    for micro in range(micros):
        columns[...] = jnp.full(columns.shape, 0.0, jnp.float32)
        rest = gates_in[micro]
        for piece in range(3):
            part = rest.astype(jnp.bfloat16).astype(jnp.float32)
            rest = rest - part
            columns[HOT_GATE + piece : HOT_GATE + piece + 1] = part[:1]
            columns[PIECE + piece * SLOT : PIECE + piece * SLOT + picks] = part[1:]
            columns[piece * SLOT + picks : (piece + 1) * SLOT] = jnp.full((SLOT - picks, held), -1.0, jnp.float32)
            for k in range(picks):
                row = piece * SLOT + k
                columns[row : row + 1] = routes_in[k, micro : micro + 1].astype(jnp.float32)
        columns[HOT_PICK : HOT_PICK + 1] = pick_in[micro : micro + 1].astype(jnp.float32)
        out, place = places[micro]
        out[place, width:] = columns[...].T.astype(jnp.bfloat16)
    for copy in copies[3:]:
        copy.wait()


def in_place(arrays):
    return [pltpu.with_memory_space_constraint(array, pltpu.HBM) for array in arrays]


def build_rows(tokens, cold_routes, hot_pick, gates, parts):
    micros, held, width = tokens.shape
    whole = pl.BlockSpec(memory_space=pltpu.VMEM)
    return pl.pallas_call(
        functools.partial(rows_body, micros=micros, parts=parts),
        in_specs=[pl.BlockSpec(memory_space=pltpu.HBM)] * 4,
        out_specs=[whole] * parts,
        out_shape=[jax.ShapeDtypeStruct((micros // parts * held, width + LANES), jnp.bfloat16)] * parts,
        scratch_shapes=[
            pltpu.VMEM((micros, gates.shape[-1], held), jnp.float32),
            pltpu.VMEM((cold_routes.shape[-1], micros, held), jnp.int32),
            pltpu.VMEM((micros, held), jnp.int32),
            pltpu.VMEM((LANES, held), jnp.float32),
            pltpu.SemaphoreType.DMA((3 + micros,)),
        ],
        compiler_params=pltpu.CompilerParams(vmem_limit_bytes=8 << 20),
        cost_estimate=pl.CostEstimate(flops=0, bytes_accessed=4 * micros * held * width, transcendentals=0),
    )(*in_place([tokens, jnp.swapaxes(gates, 1, 2), jnp.transpose(cold_routes, (2, 0, 1)), hot_pick]))


def load_body(me_ref, *refs, parts, hots, hot_parts):
    blocks, refs = refs[: 2 * parts], refs[2 * parts :]
    far, refs = refs[: 4 + hot_parts], refs[4 + hot_parts :]
    outs, near, scratch, done = refs[:2], refs[2:7], refs[7:10], refs[10]
    copies, offset = [[], [], [], []], 0

    def add(group, source, target):
        number = sum(len(waiting) for waiting in copies)
        copies[group].append(pltpu.make_async_copy(source, target, done.at[number]))

    for part in far[4:]:
        add(0, part, near[3].at[pl.ds(offset, part.shape[0])])
        offset += part.shape[0]
    units = near[0].shape[1]
    tile = tile_of(units, 256)
    for start in range(0, units, tile):
        for source, target in zip(far[:2], near[:2]):
            add(1, source.at[:, pl.ds(start, tile)], target.at[:, pl.ds(start, tile)])
    add(2, far[2], near[2])
    add(3, far[3], near[4])
    for group in copies:
        for copy in group:
            copy.start()

    def ready(group, number):
        if group == 1:
            copies[1][2 * number].wait()
            copies[1][2 * number + 1].wait()
            return
        for copy in copies[group]:
            copy.wait()

    work_body(me_ref, *blocks, *near, *outs, *scratch, parts=parts, hots=hots, ready=ready)


def work_body(me_ref, *refs, parts, hots, ready=lambda group, number: None):
    blocks, refs = refs[: 2 * parts], refs[2 * parts :]
    (gate, up, down, hot_in, hot_out), (y_mine, y_shared), (rows, hidden, hot_hidden) = refs[:5], refs[5:7], refs[7:]
    count, width = y_mine.shape
    units = gate.shape[1]
    start = 0
    for block in blocks:
        rows[start : start + block.shape[0]] = block[:, :width]
        start += block.shape[0]
    facts = jnp.concatenate([block[:, width:] for block in blocks], axis=0).astype(jnp.float32)
    lane = lax.broadcasted_iota(jnp.int32, facts.shape, 1)
    named = (facts == me_ref[0].astype(jnp.float32)) & (lane < 3 * SLOT)
    pieces = pltpu.roll(facts, LANES - PIECE, 1)
    cold_weight = jnp.sum(jnp.where(named, pieces, 0.0), axis=1, keepdims=True)
    is_hot = (lane >= HOT_GATE) & (lane < HOT_PICK)
    hot_weight = jnp.sum(jnp.where(is_hot, facts, 0.0), axis=1, keepdims=True)
    hot_pick = jnp.sum(jnp.where(lane == HOT_PICK, facts, 0.0), axis=1, keepdims=True)

    split = hot_in.shape[0] // 2
    ready(0, 0)
    both = lax.dot_general(
        rows[...], hot_in[...], (((1,), (1,)), ((), ())), preferred_element_type=jnp.float32
    )
    value = silu(both[:, :split]) * both[:, split:]
    owner = lax.broadcasted_iota(jnp.int32, value.shape, 1) // (split // hots)
    hot_hidden[...] = jnp.where(owner.astype(jnp.float32) == hot_pick, value, 0.0).astype(jnp.bfloat16)

    tile = tile_of(units, 256)
    for start in range(0, units, tile):
        cut = slice(start, start + tile)
        ready(1, start // tile)
        a = jnp.dot(rows[...], gate[:, cut], preferred_element_type=jnp.float32)
        b = jnp.dot(rows[...], up[:, cut], preferred_element_type=jnp.float32)
        hidden[:, cut] = (silu(a) * b).astype(jnp.bfloat16)
    ready(2, 0)
    ready(3, 0)
    tile = tile_of(width, 512)
    for start in range(0, width, tile):
        cut = slice(start, start + tile)
        y = cold_weight * jnp.dot(hidden[...], down[:, cut], preferred_element_type=jnp.float32)
        y = y + hot_weight * jnp.dot(hot_hidden[...], hot_out[:, cut], preferred_element_type=jnp.float32)
        y_mine[:, cut] = y[:count].astype(y_mine.dtype)
        y_shared[:, cut] = y[count:].astype(y_shared.dtype)


def work(me, mine, shared, weights, hots, bring=False):
    count, parts = sum(part.shape[0] for part in mine), len(mine)
    width, units = weights[0].shape
    whole, far = pl.BlockSpec(memory_space=pltpu.VMEM), pl.BlockSpec(memory_space=pltpu.HBM)
    out_shape = [jax.ShapeDtypeStruct((count, width), jnp.bfloat16)] * 2
    hot_units = weights[3 if bring else 4].shape[0]
    scratch = [
        pltpu.VMEM((2 * count, width), jnp.bfloat16),
        pltpu.VMEM((2 * count, units), jnp.bfloat16),
        pltpu.VMEM((2 * count, hot_units), jnp.bfloat16),
    ]
    body = functools.partial(work_body, parts=parts, hots=hots)
    if bring:
        body = functools.partial(load_body, parts=parts, hots=hots, hot_parts=len(weights) - 4)
        shapes = [w.shape for w in weights[:3]] + [(2 * hot_units, width), (hot_units, width)]
        out_shape += [jax.ShapeDtypeStruct(shape, jnp.bfloat16) for shape in shapes]
        scratch += [pltpu.SemaphoreType.DMA((len(weights) + 2 * (units // tile_of(units, 256)) - 2,))]
    return pl.pallas_call(
        body,
        in_specs=[pl.BlockSpec(memory_space=pltpu.SMEM)] + [whole] * (2 * parts) + [far if bring else whole] * len(weights),
        out_specs=[whole] * len(out_shape),
        out_shape=out_shape,
        scratch_shapes=scratch,
        compiler_params=pltpu.CompilerParams(vmem_limit_bytes=24 << 20),
        cost_estimate=pl.CostEstimate(
            flops=2 * 2 * count * width * 3 * (units + hot_units),
            bytes_accessed=2 * 4 * count * width,
            transcendentals=2 * count * units,
        ),
    )(me, *mine, *shared, *(in_place(weights) if bring else weights))


def shards(tokens, w_gate, w_up, w_down, hot_gate, hot_up, hot_down, cold_routes, hot_pick, gates):
    devices = lax.axis_size("expert")
    micros, held, width = tokens.shape
    hots, _, hot_units = hot_gate.shape
    chips = devices // 2
    around, across = ring_tables(devices)
    me = lax.axis_index("expert").astype(jnp.int32).reshape(1)

    def swap(parts):
        return [lax.ppermute(part, "expert", across) for part in parts]

    def onward(parts):
        return [lax.ppermute(part, "expert", around) for part in parts]

    rows = build_rows(tokens, cold_routes, hot_pick, gates, FIRST_PARTS)
    flat = [jnp.swapaxes(w, 1, 2).reshape(hots * hot_units, width) for w in (hot_gate, hot_up, hot_down)]
    hot_in = flat[:2] if hots * hot_units % 16 == 0 else [jnp.concatenate(flat[:2])]
    weights = (w_gate[0], w_up[0], w_down[0], flat[2], *hot_in)

    own = work(me, rows, swap(rows), weights, hots, bring=True)
    own, weights = own[:2], own[2:]
    coming, total = None, None
    mine = rows
    for step in range(1, chips):
        if step == MERGE_AT and len(mine) > 1:
            mine = [jnp.concatenate(mine)]
        mine = onward(mine)
        if step == OWN_AT:
            mine, own = lax.optimization_barrier((mine, own))
        if total is not None:
            me, total = lax.optimization_barrier((me, total))
            coming = onward(total)
        kept, given = work(me, mine, swap(mine), weights, hots)
        (taken,) = swap([given])
        parts = LAST_PARTS if step >= chips - LAST_STEPS else 1
        total = add_parts(kept, taken, coming, parts)
    coming = onward(total)
    (taken,) = swap([own[1]])
    outs = add_parts(own[0], taken, coming, len(coming))
    return jnp.concatenate(outs).reshape(micros, held, width)


def add_parts(kept, taken, coming, parts):
    size = kept.shape[0] // parts
    sums = []
    for part in range(parts):
        cut = slice(part * size, (part + 1) * size)
        total = kept[cut].astype(jnp.float32) + taken[cut].astype(jnp.float32)
        if coming is not None:
            before = coming[part] if len(coming) == parts else coming[0][cut]
            if ORDERED and sums:
                before, sums[-1] = lax.optimization_barrier((before, sums[-1]))
            total = total + before.astype(jnp.float32)
        sums.append(total.astype(jnp.bfloat16))
    return sums


def solution(mesh):
    in_specs = (
        P(None, ("groups", "expert"), None),
        P("expert", None, None),
        P("expert", None, None),
        P("expert", None, None),
        P(None, None, "expert"),
        P(None, None, "expert"),
        P(None, None, "expert"),
        P(None, ("groups", "expert"), None),
        P(None, ("groups", "expert")),
        P(None, ("groups", "expert"), None),
    )
    out_specs = P(None, ("groups", "expert"), None)
    return jax.shard_map(shards, mesh=mesh, in_specs=in_specs, out_specs=out_specs, check_vma=False)
```

time: 118 us -> 103 us (0.87)
  local copies, waits for them, and re-layouts: 11.8 us -> 0 us
  other arithmetic: 8.42 us -> 2.61 us
  Pallas kernels: 30.7 us -> 33 us
    unnamed x20 -> x0, local copies, waits for them, and re-layouts: 7.88 us -> none
    concatenate x2 -> x0, other arithmetic: 3.63 us -> none  [the longest x1 2.43 us: shards(): jnp.concatenate([w[h] for w in (hot_gate, hot_up) for h in range(hots)],...]
    pallas_call x8 -> x9, Pallas kernels: 30.7 us -> 33 us  [the longest x8 31.9 us: work(): pl.pallas_call(body, in_specs=[pl.BlockSpec(memory_space=pltpu.SMEM)] + [...]
    slice x14 -> x0, local copies, waits for them, and re-layouts: 1.55 us -> none  [the longest x2 0.78 us: shards(): w[h]]
    another operation x2 -> x0, other arithmetic: 1.5 us -> none
    concatenate x1 -> x0, local copies, waits for them, and re-layouts: 1.33 us -> none  [shards(): jnp.concatenate([tokens, facts_of(cold_routes, hot_pick, gates)], axis=-1)]
    convert_element_type x9 -> x8, other arithmetic: 3.29 us -> 2.61 us  [add_parts(): sums.append(total.astype(jnp.bfloat16))]
  transfers between devices with their start and end apart: 30 -> 30, of which waited for: 9 -> 10; matrix products, arithmetic and copies ran while one was open for 11% -> 2% of each run, Pallas kernels for 26% -> 31%
where the time goes in v1:
time: 103 us
  waiting for transfers between devices  34.9 us (34%)
  Pallas kernels  33 us (32%)
  starting transfers between devices  32 us (31%)
  other arithmetic  2.61 us (3%)
    ppermute x14, waiting for transfers between devices, onward(): return [lax.ppermute(part, 'expert', around) for part in parts]  34.9 us
    pallas_call x8, Pallas kernels, work(): pl.pallas_call(body, in_specs=[pl.BlockSpec(memory_space=pltpu.SMEM)] + [...  31.9 us
    ppermute x14, starting transfers between devices, onward(): return [lax.ppermute(part, 'expert', around) for part in parts]  28.4 us
    ppermute x16, starting transfers between devices, swap(): return [lax.ppermute(part, 'expert', across) for part in parts]  3.64 us
    convert_element_type x8, other arithmetic, add_parts(): sums.append(total.astype(jnp.bfloat16))  2.61 us
  transfers between devices with their start and end apart: 30, of which 10 were waited for; matrix products, arithmetic and copies ran while one was open for 2% of the time, Pallas kernels for 31%

profile of v1, /device:TPU:0, one launch (start us, length us, event | category | flops | bytes accessed | tf_op | source)
XLA Modules:
  0.0 102.8 jit_solution(6516048340999995065)
XLA Ops:
  1.6 2.6 %collective-permute-start = (bf16[128,2176]{1,0:T(8,128)(2,1)S(1)}, bf16[128,2176]{1,0:T(8,128)(2,1)S(1)}, u32[]{:S(2)}, u32[]{:S(2)}) collective-permute-start(bf16[128,2176]{1,0:T(8,128)(2,1)S(1)} %shard_map.100.refs_0_), channel_id=1, source_target_pairs={{0,4},{1,3},{4,8},{5,1},{8,12},{9,5},{12,14},{13,9},{14,10},{15,13... | collective-permute-start | bytes 1671176 | tf_op jit(solution)/shard_map/ppermute | solution.py:231
  4.3 6.3 %shard_map.101 = (bf16[128,2048]{1,0:T(8,128)(2,1)S(1)}, bf16[128,2048]{1,0:T(8,128)(2,1)S(1)}, bf16[2048,768]{1,0:T(8,128)(2,1)S(1)}, bf16[2048,768]{1,0:T(8,12...) custom-call(s32[1]{0:T(128)} %bitcast.2.me_ref, ...), custom_call_target="tpu_custom_call" | custom-call | flops 2717908992 | bytes 2097152 | tf_op jit(solution)/shard_map/pallas_call | solution.py:204
  13.8 3.7 %shard_map.102 = (bf16[128,2048]{1,0:T(8,128)(2,1)S(1)}, bf16[128,2048]{1,0:T(8,128)(2,1)S(1)}) custom-call(s32[1]{0:T(128)} %bitcast.2.me_ref, bf16[128,2176]{1,0:T(8,128)(2,1)S(1)} %collective-permute-done.refs_0_, bf16[128,2176]{1,0:T(8,128)(2,1)S(1)} %collective-permute-done.3.refs_1_, bf16[2048,768]{1,0:T(8,128)(2,1)S(1)} %get-tuple-element.46.refs_2_, ...), custom_call_target="tpu_custom_call" | custom-call | flops 2717908992 | bytes 2097152 | tf_op jit(solution)/shard_map/pallas_call | solution.py:204
  17.7 3.5 %collective-permute-done.5.refs_0_ = bf16[128,2176]{1,0:T(8,128)(2,1)S(1)} collective-permute-done((bf16[128,2176]{1,0:T(8,128)(2,1)S(1)}, bf16[128,2176]{1,0:T(8,128)(2,1)S(1)}, u32[]{:S(2)}, u32[]{:S(2)}) %collective-permute-start.5) | collective-permute-done | bytes 557088 | tf_op jit(solution)/shard_map/ppermute | solution.py:231
  25.1 3.7 %shard_map.103 = (bf16[128,2048]{1,0:T(8,128)(2,1)S(1)}, bf16[128,2048]{1,0:T(8,128)(2,1)S(1)}) custom-call(s32[1]{0:T(128)} %bitcast.2.me_ref, bf16[128,2176]{1,0:T(8,128)(2,1)S(1)} %collective-permute-done.5.refs_0_, bf16[128,2176]{1,0:T(8,128)(2,1)S(1)} %collective-permute-done.6.refs_1_, bf16[2048,768]{1,0:T(8,128)(2,1)S(1)} %get-tuple-element.46.refs_2_, ...), custom_call_target="tpu_custom_call" | custom-call | flops 2717908992 | bytes 2097152 | tf_op jit(solution)/shard_map/pallas_call | solution.py:204
  30.8 2.1 %collective-permute-start.13 = (bf16[128,2176]{1,0:T(8,128)(2,1)S(1)}, bf16[128,2176]{1,0:T(8,128)(2,1)S(1)}, u32[]{:S(2)}, u32[]{:S(2)}) collective-permute-start(bf16[128,2176]{1,0:T(8,128)(2,1)S(1)} %collective-permute-done.9.refs_0_), channel_id=1, source_target_pairs={{0,4},{1,3},{4,8},{5,1},{8,12},{9,5},{12,14},{13,9},{14,10},{15,13... | collective-permute-start | bytes 1671176 | tf_op jit(solution)/shard_map/ppermute | solution.py:231
  32.9 3.5 %collective-permute-done.8 = bf16[128,2048]{1,0:T(8,128)(2,1)S(1)} collective-permute-done((bf16[128,2048]{1,0:T(8,128)(2,1)S(1)}, bf16[128,2048]{1,0:T(8,128)(2,1)S(1)}, u32[]{:S(2)}, u32[]{:S(2)}) %collective-permute-start.8) | collective-permute-done | bytes 524320 | tf_op jit(solution)/shard_map/ppermute | solution.py:231
  36.7 2.3 %collective-permute-start.12 = (bf16[128,2048]{1,0:T(8,128)(2,1)S(1)}, bf16[128,2048]{1,0:T(8,128)(2,1)S(1)}, u32[]{:S(2)}, u32[]{:S(2)}) collective-permute-start(bf16[128,2048]{1,0:T(8,128)(2,1)S(1)} %add_convert_fusion.6), channel_id=1, source_target_pairs={{0,4},{1,3},{4,8},{5,1},{8,12},{9,5},{12,14},{13,9},{14,10},{15,13... | collective-permute-start | bytes 1572872 | tf_op jit(solution)/shard_map/ppermute | solution.py:231
  39.0 3.7 %shard_map.104 = (bf16[128,2048]{1,0:T(8,128)(2,1)S(1)}, bf16[128,2048]{1,0:T(8,128)(2,1)S(1)}) custom-call(s32[1]{0:T(128)} %bitcast.2.me_ref, bf16[128,2176]{1,0:T(8,128)(2,1)S(1)} %collective-permute-done.9.refs_0_, bf16[128,2176]{1,0:T(8,128)(2,1)S(1)} %collective-permute-done.10.refs_1_, bf16[2048,768]{1,0:T(8,128)(2,1)S(1)} %get-tuple-element.46.refs_2_, ...), custom_call_target="tpu_custom_call" | custom-call | flops 2717908992 | bytes 2097152 | tf_op jit(solution)/shard_map/pallas_call | solution.py:204
  44.8 3.2 %collective-permute-done.12 = bf16[128,2048]{1,0:T(8,128)(2,1)S(1)} collective-permute-done((bf16[128,2048]{1,0:T(8,128)(2,1)S(1)}, bf16[128,2048]{1,0:T(8,128)(2,1)S(1)}, u32[]{:S(2)}, u32[]{:S(2)}) %collective-permute-start.12) | collective-permute-done | bytes 524320 | tf_op jit(solution)/shard_map/ppermute | solution.py:231
  48.3 2.1 %collective-permute-start.16 = (bf16[128,2048]{1,0:T(8,128)(2,1)S(1)}, bf16[128,2048]{1,0:T(8,128)(2,1)S(1)}, u32[]{:S(2)}, u32[]{:S(2)}) collective-permute-start(bf16[128,2048]{1,0:T(8,128)(2,1)S(1)} %add_convert_fusion.5), channel_id=1, source_target_pairs={{0,4},{1,3},{4,8},{5,1},{8,12},{9,5},{12,14},{13,9},{14,10},{15,13... | collective-permute-start | bytes 1572872 | tf_op jit(solution)/shard_map/ppermute | solution.py:231
  50.4 3.7 %shard_map.105 = (bf16[128,2048]{1,0:T(8,128)(2,1)S(1)}, bf16[128,2048]{1,0:T(8,128)(2,1)S(1)}) custom-call(s32[1]{0:T(128)} %bitcast.2.me_ref, bf16[128,2176]{1,0:T(8,128)(2,1)S(1)} %collective-permute-done.13.refs_0_, bf16[128,2176]{1,0:T(8,128)(2,1)S(1)} %collective-permute-done.14.refs_1_, bf16[2048,768]{1,0:T(8,128)(2,1)S(1)} %get-tuple-element.46.refs_2_, ...), custom_call_target="tpu_custom_call" | custom-call | flops 2717908992 | bytes 2097152 | tf_op jit(solution)/shard_map/pallas_call | solution.py:204
  56.2 3.4 %collective-permute-done.16 = bf16[128,2048]{1,0:T(8,128)(2,1)S(1)} collective-permute-done((bf16[128,2048]{1,0:T(8,128)(2,1)S(1)}, bf16[128,2048]{1,0:T(8,128)(2,1)S(1)}, u32[]{:S(2)}, u32[]{:S(2)}) %collective-permute-start.16) | collective-permute-done | bytes 524320 | tf_op jit(solution)/shard_map/ppermute | solution.py:231
  59.9 2.1 %collective-permute-start.20 = (bf16[128,2048]{1,0:T(8,128)(2,1)S(1)}, bf16[128,2048]{1,0:T(8,128)(2,1)S(1)}, u32[]{:S(2)}, u32[]{:S(2)}) collective-permute-start(bf16[128,2048]{1,0:T(8,128)(2,1)S(1)} %add_convert_fusion.4), channel_id=1, source_target_pairs={{0,4},{1,3},{4,8},{5,1},{8,12},{9,5},{12,14},{13,9},{14,10},{15,13... | collective-permute-start | bytes 1572872 | tf_op jit(solution)/shard_map/ppermute | solution.py:231
  62.0 3.7 %shard_map.106 = (bf16[128,2048]{1,0:T(8,128)(2,1)S(1)}, bf16[128,2048]{1,0:T(8,128)(2,1)S(1)}) custom-call(s32[1]{0:T(128)} %bitcast.2.me_ref, bf16[128,2176]{1,0:T(8,128)(2,1)S(1)} %collective-permute-done.17.refs_0_, bf16[128,2176]{1,0:T(8,128)(2,1)S(1)} %collective-permute-done.18.refs_1_, bf16[2048,768]{1,0:T(8,128)(2,1)S(1)} %get-tuple-element.46.refs_2_, ...), custom_call_target="tpu_custom_call" | custom-call | flops 2717908992 | bytes 2097152 | tf_op jit(solution)/shard_map/pallas_call | solution.py:204
  67.8 3.4 %collective-permute-done.20 = bf16[128,2048]{1,0:T(8,128)(2,1)S(1)} collective-permute-done((bf16[128,2048]{1,0:T(8,128)(2,1)S(1)}, bf16[128,2048]{1,0:T(8,128)(2,1)S(1)}, u32[]{:S(2)}, u32[]{:S(2)}) %collective-permute-start.20) | collective-permute-done | bytes 524320 | tf_op jit(solution)/shard_map/ppermute | solution.py:231
  71.4 2.3 %collective-permute-start.24 = (bf16[128,2048]{1,0:T(8,128)(2,1)S(1)}, bf16[128,2048]{1,0:T(8,128)(2,1)S(1)}, u32[]{:S(2)}, u32[]{:S(2)}) collective-permute-start(bf16[128,2048]{1,0:T(8,128)(2,1)S(1)} %add_convert_fusion.3), channel_id=1, source_target_pairs={{0,4},{1,3},{4,8},{5,1},{8,12},{9,5},{12,14},{13,9},{14,10},{15,13... | collective-permute-start | bytes 1572872 | tf_op jit(solution)/shard_map/ppermute | solution.py:231
  73.8 3.7 %shard_map.107 = (bf16[128,2048]{1,0:T(8,128)(2,1)S(1)}, bf16[128,2048]{1,0:T(8,128)(2,1)S(1)}) custom-call(s32[1]{0:T(128)} %bitcast.2.me_ref, bf16[128,2176]{1,0:T(8,128)(2,1)S(1)} %collective-permute-done.21.refs_0_, bf16[128,2176]{1,0:T(8,128)(2,1)S(1)} %collective-permute-done.22.refs_1_, bf16[2048,768]{1,0:T(8,128)(2,1)S(1)} %get-tuple-element.46.refs_2_, ...), custom_call_target="tpu_custom_call" | custom-call | flops 2717908992 | bytes 2097152 | tf_op jit(solution)/shard_map/pallas_call | solution.py:204
  78.0 4.7 %collective-permute-done.24 = bf16[128,2048]{1,0:T(8,128)(2,1)S(1)} collective-permute-done((bf16[128,2048]{1,0:T(8,128)(2,1)S(1)}, bf16[128,2048]{1,0:T(8,128)(2,1)S(1)}, u32[]{:S(2)}, u32[]{:S(2)}) %collective-permute-start.24) | collective-permute-done | bytes 524320 | tf_op jit(solution)/shard_map/ppermute | solution.py:231
  83.0 2.1 %collective-permute-start.28 = (bf16[128,2048]{1,0:T(8,128)(2,1)S(1)}, bf16[128,2048]{1,0:T(8,128)(2,1)S(1)}, u32[]{:S(2)}, u32[]{:S(2)}) collective-permute-start(bf16[128,2048]{1,0:T(8,128)(2,1)S(1)} %add_convert_fusion.2), channel_id=1, source_target_pairs={{0,4},{1,3},{4,8},{5,1},{8,12},{9,5},{12,14},{13,9},{14,10},{15,13... | collective-permute-start | bytes 1572872 | tf_op jit(solution)/shard_map/ppermute | solution.py:231
  85.2 3.7 %shard_map.108 = (bf16[128,2048]{1,0:T(8,128)(2,1)S(1)}, bf16[128,2048]{1,0:T(8,128)(2,1)S(1)}) custom-call(s32[1]{0:T(128)} %bitcast.2.me_ref, bf16[128,2176]{1,0:T(8,128)(2,1)S(1)} %collective-permute-done.25.refs_0_, bf16[128,2176]{1,0:T(8,128)(2,1)S(1)} %collective-permute-done.26.refs_1_, bf16[2048,768]{1,0:T(8,128)(2,1)S(1)} %get-tuple-element.46.refs_2_, ...), custom_call_target="tpu_custom_call" | custom-call | flops 2717908992 | bytes 2097152 | tf_op jit(solution)/shard_map/pallas_call | solution.py:204
  89.4 2.9 %collective-permute-done.28 = bf16[128,2048]{1,0:T(8,128)(2,1)S(1)} collective-permute-done((bf16[128,2048]{1,0:T(8,128)(2,1)S(1)}, bf16[128,2048]{1,0:T(8,128)(2,1)S(1)}, u32[]{:S(2)}, u32[]{:S(2)}) %collective-permute-start.28) | collective-permute-done | bytes 524320 | tf_op jit(solution)/shard_map/ppermute | solution.py:231
  92.5 2.1 %collective-permute-start.29 = (bf16[128,2048]{1,0:T(8,128)(2,1)S(1)}, bf16[128,2048]{1,0:T(8,128)(2,1)S(1)}, u32[]{:S(2)}, u32[]{:S(2)}) collective-permute-start(bf16[128,2048]{1,0:T(8,128)(2,1)S(1)} %add_convert_fusion.1), channel_id=1, source_target_pairs={{0,4},{1,3},{4,8},{5,1},{8,12},{9,5},{12,14},{13,9},{14,10},{15,13... | collective-permute-start | bytes 1572872 | tf_op jit(solution)/shard_map/ppermute | solution.py:231
  94.6 7.1 %collective-permute-done.29 = bf16[128,2048]{1,0:T(8,128)(2,1)S(1)} collective-permute-done((bf16[128,2048]{1,0:T(8,128)(2,1)S(1)}, bf16[128,2048]{1,0:T(8,128)(2,1)S(1)}, u32[]{:S(2)}, u32[]{:S(2)}) %collective-permute-start.29) | collective-permute-done | bytes 524320 | tf_op jit(solution)/shard_map/ppermute | solution.py:231
  (53 shorter events, 21.0 us)
Async XLA Ops:
  1.6 10.1 %collective-permute-start = (bf16[128,2176]{1,0:T(8,128)(2,1)S(1)}, bf16[128,2176]{1,0:T(8,128)(2,1)S(1)}, u32[]{:S(2)}, u32[]{:S(2)}) collective-permute-start(bf16[128,2176]{1,0:T(8,128)(2,1)S(1)} %shard_map.100.refs_0_), channel_id=1, source_target_pairs={{0,4},{1,3},{4,8},{5,1},{8,12},{9,5},{12,14},{13,9},{14,10},{15,13... | collective-permute-start | bytes 1671176 | tf_op jit(solution)/shard_map/ppermute | solution.py:231
  11.7 9.5 %collective-permute-start.5 = (bf16[128,2176]{1,0:T(8,128)(2,1)S(1)}, bf16[128,2176]{1,0:T(8,128)(2,1)S(1)}, u32[]{:S(2)}, u32[]{:S(2)}) collective-permute-start(bf16[128,2176]{1,0:T(8,128)(2,1)S(1)} %collective-permute-done.refs_0_), channel_id=1, source_target_pairs={{0,4},{1,3},{4,8},{5,1},{8,12},{9,5},{12,14},{13,9},{14,10},{15,13... | collective-permute-start | bytes 1671176 | tf_op jit(solution)/shard_map/ppermute | solution.py:231
  17.5 5.9 %collective-permute-start.4 = (bf16[128,2048]{1,0:T(8,128)(2,1)S(1)}, bf16[128,2048]{1,0:T(8,128)(2,1)S(1)}, u32[]{:S(2)}, u32[]{:S(2)}) collective-permute-start(bf16[128,2048]{1,0:T(8,128)(2,1)S(1)} %get-tuple-element.52), channel_id=1, source_target_pairs={{0,1},{1,0},{2,3},{3,2},{4,5},{5,4},{6,7},{7,6},{8,9},{9,8},{10,11... | collective-permute-start | bytes 1572872 | tf_op jit(solution)/shard_map/ppermute | solution.py:228
  21.3 9.5 %collective-permute-start.9 = (bf16[128,2176]{1,0:T(8,128)(2,1)S(1)}, bf16[128,2176]{1,0:T(8,128)(2,1)S(1)}, u32[]{:S(2)}, u32[]{:S(2)}) collective-permute-start(bf16[128,2176]{1,0:T(8,128)(2,1)S(1)} %collective-permute-done.5.refs_0_), channel_id=1, source_target_pairs={{0,4},{1,3},{4,8},{5,1},{8,12},{9,5},{12,14},{13,9},{14,10},{15,13... | collective-permute-start | bytes 1671176 | tf_op jit(solution)/shard_map/ppermute | solution.py:231
  23.5 12.9 %collective-permute-start.8 = (bf16[128,2048]{1,0:T(8,128)(2,1)S(1)}, bf16[128,2048]{1,0:T(8,128)(2,1)S(1)}, u32[]{:S(2)}, u32[]{:S(2)}) collective-permute-start(bf16[128,2048]{1,0:T(8,128)(2,1)S(1)} %add_convert_fusion.7), channel_id=1, source_target_pairs={{0,4},{1,3},{4,8},{5,1},{8,12},{9,5},{12,14},{13,9},{14,10},{15,13... | collective-permute-start | bytes 1572872 | tf_op jit(solution)/shard_map/ppermute | solution.py:231
  28.8 7.6 %collective-permute-start.7 = (bf16[128,2048]{1,0:T(8,128)(2,1)S(1)}, bf16[128,2048]{1,0:T(8,128)(2,1)S(1)}, u32[]{:S(2)}, u32[]{:S(2)}) collective-permute-start(bf16[128,2048]{1,0:T(8,128)(2,1)S(1)} %get-tuple-element.55), channel_id=1, source_target_pairs={{0,1},{1,0},{2,3},{3,2},{4,5},{5,4},{6,7},{7,6},{8,9},{9,8},{10,11... | collective-permute-start | bytes 1572872 | tf_op jit(solution)/shard_map/ppermute | solution.py:228
  30.8 8.2 %collective-permute-start.10 = (bf16[128,2176]{1,0:T(8,128)(2,1)S(1)}, bf16[128,2176]{1,0:T(8,128)(2,1)S(1)}, u32[]{:S(2)}, u32[]{:S(2)}) collective-permute-start(bf16[128,2176]{1,0:T(8,128)(2,1)S(1)} %collective-permute-done.9.refs_0_), channel_id=1, source_target_pairs={{0,1},{1,0},{2,3},{3,2},{4,5},{5,4},{6,7},{7,6},{8,9},{9,8},{10,11... | collective-permute-start | bytes 1671176 | tf_op jit(solution)/shard_map/ppermute | solution.py:228
  30.8 11.9 %collective-permute-start.13 = (bf16[128,2176]{1,0:T(8,128)(2,1)S(1)}, bf16[128,2176]{1,0:T(8,128)(2,1)S(1)}, u32[]{:S(2)}, u32[]{:S(2)}) collective-permute-start(bf16[128,2176]{1,0:T(8,128)(2,1)S(1)} %collective-permute-done.9.refs_0_), channel_id=1, source_target_pairs={{0,4},{1,3},{4,8},{5,1},{8,12},{9,5},{12,14},{13,9},{14,10},{15,13... | collective-permute-start | bytes 1671176 | tf_op jit(solution)/shard_map/ppermute | solution.py:231
  36.7 11.3 %collective-permute-start.12 = (bf16[128,2048]{1,0:T(8,128)(2,1)S(1)}, bf16[128,2048]{1,0:T(8,128)(2,1)S(1)}, u32[]{:S(2)}, u32[]{:S(2)}) collective-permute-start(bf16[128,2048]{1,0:T(8,128)(2,1)S(1)} %add_convert_fusion.6), channel_id=1, source_target_pairs={{0,4},{1,3},{4,8},{5,1},{8,12},{9,5},{12,14},{13,9},{14,10},{15,13... | collective-permute-start | bytes 1572872 | tf_op jit(solution)/shard_map/ppermute | solution.py:231
  42.7 7.7 %collective-permute-start.14 = (bf16[128,2176]{1,0:T(8,128)(2,1)S(1)}, bf16[128,2176]{1,0:T(8,128)(2,1)S(1)}, u32[]{:S(2)}, u32[]{:S(2)}) collective-permute-start(bf16[128,2176]{1,0:T(8,128)(2,1)S(1)} %collective-permute-done.13.refs_0_), channel_id=1, source_target_pairs={{0,1},{1,0},{2,3},{3,2},{4,5},{5,4},{6,7},{7,6},{8,9},{9,8},{10,11... | collective-permute-start | bytes 1671176 | tf_op jit(solution)/shard_map/ppermute | solution.py:228
  43.2 10.9 %collective-permute-start.17 = (bf16[128,2176]{1,0:T(8,128)(2,1)S(1)}, bf16[128,2176]{1,0:T(8,128)(2,1)S(1)}, u32[]{:S(2)}, u32[]{:S(2)}) collective-permute-start(bf16[128,2176]{1,0:T(8,128)(2,1)S(1)} %collective-permute-done.13.refs_0_), channel_id=1, source_target_pairs={{0,4},{1,3},{4,8},{5,1},{8,12},{9,5},{12,14},{13,9},{14,10},{15,13... | collective-permute-start | bytes 1671176 | tf_op jit(solution)/shard_map/ppermute | solution.py:231
  48.3 11.3 %collective-permute-start.16 = (bf16[128,2048]{1,0:T(8,128)(2,1)S(1)}, bf16[128,2048]{1,0:T(8,128)(2,1)S(1)}, u32[]{:S(2)}, u32[]{:S(2)}) collective-permute-start(bf16[128,2048]{1,0:T(8,128)(2,1)S(1)} %add_convert_fusion.5), channel_id=1, source_target_pairs={{0,4},{1,3},{4,8},{5,1},{8,12},{9,5},{12,14},{13,9},{14,10},{15,13... | collective-permute-start | bytes 1572872 | tf_op jit(solution)/shard_map/ppermute | solution.py:231
  54.1 5.5 %collective-permute-start.15 = (bf16[128,2048]{1,0:T(8,128)(2,1)S(1)}, bf16[128,2048]{1,0:T(8,128)(2,1)S(1)}, u32[]{:S(2)}, u32[]{:S(2)}) collective-permute-start(bf16[128,2048]{1,0:T(8,128)(2,1)S(1)} %get-tuple-element.63), channel_id=1, source_target_pairs={{0,1},{1,0},{2,3},{3,2},{4,5},{5,4},{6,7},{7,6},{8,9},{9,8},{10,11... | collective-permute-start | bytes 1572872 | tf_op jit(solution)/shard_map/ppermute | solution.py:228
  54.2 7.8 %collective-permute-start.18 = (bf16[128,2176]{1,0:T(8,128)(2,1)S(1)}, bf16[128,2176]{1,0:T(8,128)(2,1)S(1)}, u32[]{:S(2)}, u32[]{:S(2)}) collective-permute-start(bf16[128,2176]{1,0:T(8,128)(2,1)S(1)} %collective-permute-done.17.refs_0_), channel_id=1, source_target_pairs={{0,1},{1,0},{2,3},{3,2},{4,5},{5,4},{6,7},{7,6},{8,9},{9,8},{10,11... | collective-permute-start | bytes 1671176 | tf_op jit(solution)/shard_map/ppermute | solution.py:228
  54.6 11.1 %collective-permute-start.21 = (bf16[128,2176]{1,0:T(8,128)(2,1)S(1)}, bf16[128,2176]{1,0:T(8,128)(2,1)S(1)}, u32[]{:S(2)}, u32[]{:S(2)}) collective-permute-start(bf16[128,2176]{1,0:T(8,128)(2,1)S(1)} %collective-permute-done.17.refs_0_), channel_id=1, source_target_pairs={{0,4},{1,3},{4,8},{5,1},{8,12},{9,5},{12,14},{13,9},{14,10},{15,13... | collective-permute-start | bytes 1671176 | tf_op jit(solution)/shard_map/ppermute | solution.py:231
  59.9 11.3 %collective-permute-start.20 = (bf16[128,2048]{1,0:T(8,128)(2,1)S(1)}, bf16[128,2048]{1,0:T(8,128)(2,1)S(1)}, u32[]{:S(2)}, u32[]{:S(2)}) collective-permute-start(bf16[128,2048]{1,0:T(8,128)(2,1)S(1)} %add_convert_fusion.4), channel_id=1, source_target_pairs={{0,4},{1,3},{4,8},{5,1},{8,12},{9,5},{12,14},{13,9},{14,10},{15,13... | collective-permute-start | bytes 1572872 | tf_op jit(solution)/shard_map/ppermute | solution.py:231
  65.7 5.5 %collective-permute-start.19 = (bf16[128,2048]{1,0:T(8,128)(2,1)S(1)}, bf16[128,2048]{1,0:T(8,128)(2,1)S(1)}, u32[]{:S(2)}, u32[]{:S(2)}) collective-permute-start(bf16[128,2048]{1,0:T(8,128)(2,1)S(1)} %get-tuple-element.67), channel_id=1, source_target_pairs={{0,1},{1,0},{2,3},{3,2},{4,5},{5,4},{6,7},{7,6},{8,9},{9,8},{10,11... | collective-permute-start | bytes 1572872 | tf_op jit(solution)/shard_map/ppermute | solution.py:228
  65.7 8.1 %collective-permute-start.22 = (bf16[128,2176]{1,0:T(8,128)(2,1)S(1)}, bf16[128,2176]{1,0:T(8,128)(2,1)S(1)}, u32[]{:S(2)}, u32[]{:S(2)}) collective-permute-start(bf16[128,2176]{1,0:T(8,128)(2,1)S(1)} %collective-permute-done.21.refs_0_), channel_id=1, source_target_pairs={{0,1},{1,0},{2,3},{3,2},{4,5},{5,4},{6,7},{7,6},{8,9},{9,8},{10,11... | collective-permute-start | bytes 1671176 | tf_op jit(solution)/shard_map/ppermute | solution.py:228
  66.2 11.3 %collective-permute-start.25 = (bf16[128,2176]{1,0:T(8,128)(2,1)S(1)}, bf16[128,2176]{1,0:T(8,128)(2,1)S(1)}, u32[]{:S(2)}, u32[]{:S(2)}) collective-permute-start(bf16[128,2176]{1,0:T(8,128)(2,1)S(1)} %collective-permute-done.21.refs_0_), channel_id=1, source_target_pairs={{0,4},{1,3},{4,8},{5,1},{8,12},{9,5},{12,14},{13,9},{14,10},{15,13... | collective-permute-start | bytes 1671176 | tf_op jit(solution)/shard_map/ppermute | solution.py:231
  71.4 11.3 %collective-permute-start.24 = (bf16[128,2048]{1,0:T(8,128)(2,1)S(1)}, bf16[128,2048]{1,0:T(8,128)(2,1)S(1)}, u32[]{:S(2)}, u32[]{:S(2)}) collective-permute-start(bf16[128,2048]{1,0:T(8,128)(2,1)S(1)} %add_convert_fusion.3), channel_id=1, source_target_pairs={{0,4},{1,3},{4,8},{5,1},{8,12},{9,5},{12,14},{13,9},{14,10},{15,13... | collective-permute-start | bytes 1572872 | tf_op jit(solution)/shard_map/ppermute | solution.py:231
  77.5 7.6 %collective-permute-start.26 = (bf16[128,2176]{1,0:T(8,128)(2,1)S(1)}, bf16[128,2176]{1,0:T(8,128)(2,1)S(1)}, u32[]{:S(2)}, u32[]{:S(2)}) collective-permute-start(bf16[128,2176]{1,0:T(8,128)(2,1)S(1)} %collective-permute-done.25.refs_0_), channel_id=1, source_target_pairs={{0,1},{1,0},{2,3},{3,2},{4,5},{5,4},{6,7},{7,6},{8,9},{9,8},{10,11... | collective-permute-start | bytes 1671176 | tf_op jit(solution)/shard_map/ppermute | solution.py:228
  83.0 9.2 %collective-permute-start.28 = (bf16[128,2048]{1,0:T(8,128)(2,1)S(1)}, bf16[128,2048]{1,0:T(8,128)(2,1)S(1)}, u32[]{:S(2)}, u32[]{:S(2)}) collective-permute-start(bf16[128,2048]{1,0:T(8,128)(2,1)S(1)} %add_convert_fusion.2), channel_id=1, source_target_pairs={{0,4},{1,3},{4,8},{5,1},{8,12},{9,5},{12,14},{13,9},{14,10},{15,13... | collective-permute-start | bytes 1572872 | tf_op jit(solution)/shard_map/ppermute | solution.py:231
  88.9 5.7 %collective-permute-start.2 = (bf16[128,2048]{1,0:T(8,128)(2,1)S(1)}, bf16[128,2048]{1,0:T(8,128)(2,1)S(1)}, u32[]{:S(2)}, u32[]{:S(2)}) collective-permute-start(bf16[128,2048]{1,0:T(8,128)(2,1)S(1)} %get-tuple-element.44), channel_id=1, source_target_pairs={{0,1},{1,0},{2,3},{3,2},{4,5},{5,4},{6,7},{7,6},{8,9},{9,8},{10,11... | collective-permute-start | bytes 1572872 | tf_op jit(solution)/shard_map/ppermute | solution.py:228
  92.5 9.2 %collective-permute-start.29 = (bf16[128,2048]{1,0:T(8,128)(2,1)S(1)}, bf16[128,2048]{1,0:T(8,128)(2,1)S(1)}, u32[]{:S(2)}, u32[]{:S(2)}) collective-permute-start(bf16[128,2048]{1,0:T(8,128)(2,1)S(1)} %add_convert_fusion.1), channel_id=1, source_target_pairs={{0,4},{1,3},{4,8},{5,1},{8,12},{9,5},{12,14},{13,9},{14,10},{15,13... | collective-permute-start | bytes 1572872 | tf_op jit(solution)/shard_map/ppermute | solution.py:231
  (6 other events, 23.2 us)

commit v2 on v1

v2 whole, which is shorter than its diff:
```python
import functools

import jax
import jax.numpy as jnp
from jax import lax
from jax.experimental import pallas as pl
from jax.experimental.pallas import tpu as pltpu
from jax.sharding import PartitionSpec as P

LANES = 128


def ring_tables(devices):
    chips = devices // 2
    ring = list(range(0, chips, 2)) + list(range(chips - 1, 0, -2))
    around = []
    for place in range(chips):
        following, preceding = ring[(place + 1) % chips], ring[place - 1]
        around.append((2 * ring[place], 2 * following))
        around.append((2 * ring[place] + 1, 2 * preceding + 1))
    across = [(device, device ^ 1) for device in range(devices)]
    return around, across


def tile_of(size, most):
    tile = most
    while size % tile:
        tile //= 2
    return tile


def silu(value):
    return value / (1.0 + jnp.exp(-value))


def rows_body(tokens, gates, routes, pick, out, tokens_in, gates_in, routes_in, pick_in, columns, done, *, micros):
    held, width = tokens.shape[1:]
    count, slots = micros * held, gates.shape[1]
    group = 4 * slots
    depth = count * group // LANES
    pairs = [(gates, gates_in), (routes, routes_in), (pick, pick_in)]
    pairs += [(tokens.at[micro], tokens_in.at[pl.ds(micro * held, held)]) for micro in range(micros)]
    copies = [pltpu.make_async_copy(*pair, done.at[number]) for number, pair in enumerate(pairs)]
    for copy in copies:
        copy.start()
    for copy in copies[:3]:
        copy.wait()
    for micro in range(micros):
        rest = gates_in[micro]
        pieces = []
        for _ in range(3):
            pieces.append(rest.astype(jnp.bfloat16).astype(jnp.float32))
            rest = rest - pieces[-1]
        for part in range(held // depth):
            start = (micro * (held // depth) + part) * group
            cut = slice(part * depth, (part + 1) * depth)
            for k in range(slots - 1):
                columns[start + k : start + k + 1] = routes_in[k, micro : micro + 1, cut].astype(jnp.float32)
            columns[start + slots - 1 : start + slots] = pick_in[micro : micro + 1, cut].astype(jnp.float32)
            for number, piece in enumerate(pieces):
                columns[start + (number + 1) * slots : start + (number + 2) * slots] = piece[:, cut]
    out[width // LANES * count :] = columns[...].T.astype(jnp.bfloat16)
    for copy in copies[3:]:
        copy.wait()
    for block in range(width // LANES):
        out[block * count : (block + 1) * count] = tokens_in[:, block * LANES : (block + 1) * LANES]


def in_place(arrays):
    return [pltpu.with_memory_space_constraint(array, pltpu.HBM) for array in arrays]


def build_rows(tokens, cold_routes, hot_pick, gates):
    micros, held, width = tokens.shape
    slots, count = gates.shape[-1], micros * held
    depth = count * 4 * slots // LANES
    return pl.pallas_call(
        functools.partial(rows_body, micros=micros),
        in_specs=[pl.BlockSpec(memory_space=pltpu.HBM)] * 4,
        out_specs=pl.BlockSpec(memory_space=pltpu.VMEM),
        out_shape=jax.ShapeDtypeStruct((width // LANES * count + depth, LANES), jnp.bfloat16),
        scratch_shapes=[
            pltpu.VMEM((count, width), jnp.bfloat16),
            pltpu.VMEM((micros, slots, held), jnp.float32),
            pltpu.VMEM((slots - 1, micros, held), jnp.int32),
            pltpu.VMEM((micros, held), jnp.int32),
            pltpu.VMEM((LANES, depth), jnp.float32),
            pltpu.SemaphoreType.DMA((3 + micros,)),
        ],
        compiler_params=pltpu.CompilerParams(vmem_limit_bytes=8 << 20),
        cost_estimate=pl.CostEstimate(flops=0, bytes_accessed=4 * micros * held * width, transcendentals=0),
    )(*in_place([tokens, jnp.swapaxes(gates, 1, 2), jnp.transpose(cold_routes, (2, 0, 1)), hot_pick]))


def load_body(me_ref, *refs, slots, hots, hot_parts):
    blocks, refs = refs[:2], refs[2:]
    far, refs = refs[: 4 + hot_parts], refs[4 + hot_parts :]
    outs, near, scratch, done = refs[:2], refs[2:7], refs[7:10], refs[10]
    copies, offset = [[], [], [], []], 0

    def add(group, source, target):
        number = sum(len(waiting) for waiting in copies)
        copies[group].append(pltpu.make_async_copy(source, target, done.at[number]))

    for part in far[4:]:
        add(0, part, near[3].at[pl.ds(offset, part.shape[0])])
        offset += part.shape[0]
    units = near[0].shape[1]
    tile = tile_of(units, 256)
    for start in range(0, units, tile):
        for source, target in zip(far[:2], near[:2]):
            add(1, source.at[:, pl.ds(start, tile)], target.at[:, pl.ds(start, tile)])
    add(2, far[2], near[2])
    add(3, far[3], near[4])
    for group in copies:
        for copy in group:
            copy.start()

    def ready(group, number):
        if group == 1:
            copies[1][2 * number].wait()
            copies[1][2 * number + 1].wait()
            return
        for copy in copies[group]:
            copy.wait()

    work_body(me_ref, *blocks, *near, *outs, *scratch, slots=slots, hots=hots, ready=ready)


def work_body(me_ref, *refs, slots, hots, ready=lambda group, number: None):
    blocks, refs = refs[:2], refs[2:]
    (gate, up, down, hot_in, hot_out), (y_mine, y_shared), (rows, hidden, hot_hidden) = refs[:5], refs[5:7], refs[7:]
    count, width = y_mine.shape
    units = gate.shape[1]
    group = 4 * slots
    facts = []
    for number, block in enumerate(blocks):
        for column in range(width // LANES):
            place = slice(column * LANES, (column + 1) * LANES)
            rows[number * count : (number + 1) * count, place] = block[column * count : (column + 1) * count]
        packed = block[width // LANES * count :].astype(jnp.float32)
        facts += [pltpu.roll(packed, (LANES - start) % LANES, 1) if start else packed for start in range(0, LANES, group)]
    facts = jnp.concatenate(facts, axis=0)
    lane = lax.broadcasted_iota(jnp.int32, facts.shape, 1)
    named = (facts == me_ref[0].astype(jnp.float32)) & (lane < slots - 1)
    pieces = [pltpu.roll(facts, LANES - slots * number - 1, 1) for number in (1, 2, 3)]
    cold_weight = jnp.sum(jnp.where(named, pieces[0] + pieces[1] + pieces[2], 0.0), axis=1, keepdims=True)
    is_hot = (lane == slots) | (lane == 2 * slots) | (lane == 3 * slots)
    hot_weight = jnp.sum(jnp.where(is_hot, facts, 0.0), axis=1, keepdims=True)
    hot_pick = jnp.sum(jnp.where(lane == slots - 1, facts, 0.0), axis=1, keepdims=True)

    split = hot_in.shape[0] // 2
    ready(0, 0)
    both = lax.dot_general(
        rows[...], hot_in[...], (((1,), (1,)), ((), ())), preferred_element_type=jnp.float32
    )
    value = silu(both[:, :split]) * both[:, split:]
    owner = lax.broadcasted_iota(jnp.int32, value.shape, 1) // (split // hots)
    hot_hidden[...] = jnp.where(owner.astype(jnp.float32) == hot_pick, value, 0.0).astype(jnp.bfloat16)

    tile = tile_of(units, 256)
    for start in range(0, units, tile):
        cut = slice(start, start + tile)
        ready(1, start // tile)
        a = jnp.dot(rows[...], gate[:, cut], preferred_element_type=jnp.float32)
        b = jnp.dot(rows[...], up[:, cut], preferred_element_type=jnp.float32)
        hidden[:, cut] = (silu(a) * b).astype(jnp.bfloat16)
    ready(2, 0)
    ready(3, 0)
    tile = tile_of(width, 512)
    for start in range(0, width, tile):
        cut = slice(start, start + tile)
        y = cold_weight * jnp.dot(hidden[...], down[:, cut], preferred_element_type=jnp.float32)
        y = y + hot_weight * jnp.dot(hot_hidden[...], hot_out[:, cut], preferred_element_type=jnp.float32)
        y_mine[:, cut] = y[:count].astype(y_mine.dtype)
        y_shared[:, cut] = y[count:].astype(y_shared.dtype)


def work(me, mine, shared, weights, slots, hots, bring=False):
    width, units = weights[0].shape
    count = mine.shape[0] * LANES // (width + 4 * slots)
    whole, far = pl.BlockSpec(memory_space=pltpu.VMEM), pl.BlockSpec(memory_space=pltpu.HBM)
    out_shape = [jax.ShapeDtypeStruct((count, width), jnp.bfloat16)] * 2
    hot_units = weights[3 if bring else 4].shape[0]
    scratch = [
        pltpu.VMEM((2 * count, width), jnp.bfloat16),
        pltpu.VMEM((2 * count, units), jnp.bfloat16),
        pltpu.VMEM((2 * count, hot_units), jnp.bfloat16),
    ]
    body = functools.partial(work_body, slots=slots, hots=hots)
    if bring:
        body = functools.partial(load_body, slots=slots, hots=hots, hot_parts=len(weights) - 4)
        shapes = [w.shape for w in weights[:3]] + [(2 * hot_units, width), (hot_units, width)]
        out_shape += [jax.ShapeDtypeStruct(shape, jnp.bfloat16) for shape in shapes]
        scratch += [pltpu.SemaphoreType.DMA((len(weights) + 2 * (units // tile_of(units, 256)) - 2,))]
    return pl.pallas_call(
        body,
        in_specs=[pl.BlockSpec(memory_space=pltpu.SMEM)] + [whole] * 2 + [far if bring else whole] * len(weights),
        out_specs=[whole] * len(out_shape),
        out_shape=out_shape,
        scratch_shapes=scratch,
        compiler_params=pltpu.CompilerParams(vmem_limit_bytes=24 << 20),
        cost_estimate=pl.CostEstimate(
            flops=2 * 2 * count * width * 3 * (units + hot_units),
            bytes_accessed=2 * 4 * count * width,
            transcendentals=2 * count * units,
        ),
    )(me, mine, shared, *(in_place(weights) if bring else weights))


def shards(tokens, w_gate, w_up, w_down, hot_gate, hot_up, hot_down, cold_routes, hot_pick, gates):
    devices = lax.axis_size("expert")
    micros, held, width = tokens.shape
    hots, _, hot_units = hot_gate.shape
    chips = devices // 2
    around, across = ring_tables(devices)
    me = lax.axis_index("expert").astype(jnp.int32).reshape(1)

    def swap(x):
        return lax.ppermute(x, "expert", across)

    def onward(x):
        return lax.ppermute(x, "expert", around)

    rows = build_rows(tokens, cold_routes, hot_pick, gates)
    flat = [jnp.swapaxes(w, 1, 2).reshape(hots * hot_units, width) for w in (hot_gate, hot_up, hot_down)]
    hot_in = flat[:2] if hots * hot_units % 16 == 0 else [jnp.concatenate(flat[:2])]
    weights = (w_gate[0], w_up[0], w_down[0], flat[2], *hot_in)
    slots = gates.shape[-1]

    own = work(me, rows, swap(rows), weights, slots, hots, bring=True)
    own, weights = own[:2], own[2:]
    coming = None
    mine = rows
    for step in range(1, chips):
        mine = onward(mine)
        if step == 1:
            mine, own = lax.optimization_barrier((mine, own))
        kept, given = work(me, mine, swap(mine), weights, slots, hots)
        total = kept.astype(jnp.float32) + swap(given).astype(jnp.float32)
        if coming is not None:
            total = total + coming.astype(jnp.float32)
        coming = onward(total.astype(jnp.bfloat16))
    total = own[0].astype(jnp.float32) + swap(own[1]).astype(jnp.float32) + coming.astype(jnp.float32)
    return total.astype(jnp.bfloat16).reshape(micros, held, width)


def solution(mesh):
    in_specs = (
        P(None, ("groups", "expert"), None),
        P("expert", None, None),
        P("expert", None, None),
        P("expert", None, None),
        P(None, None, "expert"),
        P(None, None, "expert"),
        P(None, None, "expert"),
        P(None, ("groups", "expert"), None),
        P(None, ("groups", "expert")),
        P(None, ("groups", "expert"), None),
    )
    out_specs = P(None, ("groups", "expert"), None)
    return jax.shard_map(shards, mesh=mesh, in_specs=in_specs, out_specs=out_specs, check_vma=False)
```

time: 103 us -> 101 us (0.981)
  waiting for transfers between devices: 34.9 us -> 32.3 us
    ppermute x30, waiting for transfers between devices: 34.9 us -> 32.3 us  [the longest x14 32.3 us: onward(): return lax.ppermute(x, 'expert', around)]
  transfers between devices with their start and end apart: 30 -> 30, of which waited for: 10 -> 10; matrix products, arithmetic and copies ran while one was open for 2% -> 2% of each run, Pallas kernels for 31% -> 32%
where the time goes in v2:
time: 101 us
  Pallas kernels  33.8 us (33%)
  waiting for transfers between devices  32.3 us (32%)
  starting transfers between devices  32 us (32%)
  other arithmetic  2.61 us (3%)
    pallas_call x8, Pallas kernels, work(): pl.pallas_call(body, in_specs=[pl.BlockSpec(memory_space=pltpu.SMEM)] + [...  32.6 us
    ppermute x14, waiting for transfers between devices, onward(): return lax.ppermute(x, 'expert', around)  32.3 us
    ppermute x14, starting transfers between devices, onward(): return lax.ppermute(x, 'expert', around)  28.4 us
    ppermute x16, starting transfers between devices, swap(): return lax.ppermute(x, 'expert', across)  3.64 us
  transfers between devices with their start and end apart: 30, of which 10 were waited for; matrix products, arithmetic and copies ran while one was open for 2% of the time, Pallas kernels for 32%

profile of v2, /device:TPU:0, one launch (start us, length us, event | category | flops | bytes accessed | tf_op | source)
XLA Modules:
  0.0 101.0 jit_solution(4888497498172493303)
XLA Ops:
  1.7 2.6 %collective-permute-start = (bf16[2080,128]{1,0:T(8,128)(2,1)S(1)}, bf16[2080,128]{1,0:T(8,128)(2,1)S(1)}, u32[]{:S(2)}, u32[]{:S(2)}) collective-permute-start(bf16[2080,128]{1,0:T(8,128)(2,1)S(1)} %shard_map.100.refs_0_), channel_id=1, source_target_pairs={{0,4},{1,3},{4,8},{5,1},{8,12},{9,5},{12,14},{13,9},{14,10},{15,13... | collective-permute-start | bytes 1597448 | tf_op jit(solution)/shard_map/ppermute | solution.py:223
  4.4 6.6 %shard_map.101 = (bf16[128,2048]{1,0:T(8,128)(2,1)S(1)}, bf16[128,2048]{1,0:T(8,128)(2,1)S(1)}, bf16[2048,768]{1,0:T(8,128)(2,1)S(1)}, bf16[2048,768]{1,0:T(8,12...) custom-call(s32[1]{0:T(128)} %bitcast.2.me_ref, ...), custom_call_target="tpu_custom_call" | custom-call | flops 2717908992 | bytes 2097152 | tf_op jit(solution)/shard_map/pallas_call | solution.py:196
  11.6 2.1 %collective-permute-start.3 = (bf16[2080,128]{1,0:T(8,128)(2,1)S(1)}, bf16[2080,128]{1,0:T(8,128)(2,1)S(1)}, u32[]{:S(2)}, u32[]{:S(2)}) collective-permute-start(bf16[2080,128]{1,0:T(8,128)(2,1)S(1)} %collective-permute-done.refs_0_), channel_id=1, source_target_pairs={{0,4},{1,3},{4,8},{5,1},{8,12},{9,5},{12,14},{13,9},{14,10},{15,13... | collective-permute-start | bytes 1597448 | tf_op jit(solution)/shard_map/ppermute | solution.py:223
  13.7 3.7 %shard_map.108 = (bf16[128,2048]{1,0:T(8,128)(2,1)S(1)}, bf16[128,2048]{1,0:T(8,128)(2,1)S(1)}) custom-call(s32[1]{0:T(128)} %bitcast.2.me_ref, bf16[2080,128]{1,0:T(8,128)(2,1)S(1)} %collective-permute-done.refs_0_, bf16[2080,128]{1,0:T(8,128)(2,1)S(1)} %collective-permute-done.21.refs_1_, bf16[2048,768]{1,0:T(8,128)(2,1)S(1)} %get-tuple-element.34.refs_2_, ...), custom_call_target="tpu_custom_call" | custom-call | flops 2717908992 | bytes 2097152 | tf_op jit(solution)/shard_map/pallas_call | solution.py:196
  17.6 3.2 %collective-permute-done.3.refs_0_ = bf16[2080,128]{1,0:T(8,128)(2,1)S(1)} collective-permute-done((bf16[2080,128]{1,0:T(8,128)(2,1)S(1)}, bf16[2080,128]{1,0:T(8,128)(2,1)S(1)}, u32[]{:S(2)}, u32[]{:S(2)}) %collective-permute-start.3) | collective-permute-done | bytes 532512 | tf_op jit(solution)/shard_map/ppermute | solution.py:223
  24.7 3.7 %shard_map.107 = (bf16[128,2048]{1,0:T(8,128)(2,1)S(1)}, bf16[128,2048]{1,0:T(8,128)(2,1)S(1)}) custom-call(s32[1]{0:T(128)} %bitcast.2.me_ref, bf16[2080,128]{1,0:T(8,128)(2,1)S(1)} %collective-permute-done.3.refs_0_, bf16[2080,128]{1,0:T(8,128)(2,1)S(1)} %collective-permute-done.19.refs_1_, bf16[2048,768]{1,0:T(8,128)(2,1)S(1)} %get-tuple-element.34.refs_2_, ...), custom_call_target="tpu_custom_call" | custom-call | flops 2717908992 | bytes 2097152 | tf_op jit(solution)/shard_map/pallas_call | solution.py:196
  32.2 3.5 %collective-permute-done.23 = bf16[128,2048]{1,0:T(8,128)(2,1)S(1)} collective-permute-done((bf16[128,2048]{1,0:T(8,128)(2,1)S(1)}, bf16[128,2048]{1,0:T(8,128)(2,1)S(1)}, u32[]{:S(2)}, u32[]{:S(2)}) %collective-permute-start.23) | collective-permute-done | bytes 524320 | tf_op jit(solution)/shard_map/ppermute | solution.py:223
  36.0 2.3 %collective-permute-start.24 = (bf16[128,2048]{1,0:T(8,128)(2,1)S(1)}, bf16[128,2048]{1,0:T(8,128)(2,1)S(1)}, u32[]{:S(2)}, u32[]{:S(2)}) collective-permute-start(bf16[128,2048]{1,0:T(8,128)(2,1)S(1)} %add_convert_fusion.6), channel_id=1, source_target_pairs={{0,4},{1,3},{4,8},{5,1},{8,12},{9,5},{12,14},{13,9},{14,10},{15,13... | collective-permute-start | bytes 1572872 | tf_op jit(solution)/shard_map/ppermute | solution.py:223
  38.3 3.7 %shard_map.106 = (bf16[128,2048]{1,0:T(8,128)(2,1)S(1)}, bf16[128,2048]{1,0:T(8,128)(2,1)S(1)}) custom-call(s32[1]{0:T(128)} %bitcast.2.me_ref, bf16[2080,128]{1,0:T(8,128)(2,1)S(1)} %collective-permute-done.4.refs_0_, bf16[2080,128]{1,0:T(8,128)(2,1)S(1)} %collective-permute-done.17.refs_1_, bf16[2048,768]{1,0:T(8,128)(2,1)S(1)} %get-tuple-element.34.refs_2_, ...), custom_call_target="tpu_custom_call" | custom-call | flops 2717908992 | bytes 2097152 | tf_op jit(solution)/shard_map/pallas_call | solution.py:196
  44.2 2.9 %collective-permute-done.24 = bf16[128,2048]{1,0:T(8,128)(2,1)S(1)} collective-permute-done((bf16[128,2048]{1,0:T(8,128)(2,1)S(1)}, bf16[128,2048]{1,0:T(8,128)(2,1)S(1)}, u32[]{:S(2)}, u32[]{:S(2)}) %collective-permute-start.24) | collective-permute-done | bytes 524320 | tf_op jit(solution)/shard_map/ppermute | solution.py:223
  47.3 2.1 %collective-permute-start.25 = (bf16[128,2048]{1,0:T(8,128)(2,1)S(1)}, bf16[128,2048]{1,0:T(8,128)(2,1)S(1)}, u32[]{:S(2)}, u32[]{:S(2)}) collective-permute-start(bf16[128,2048]{1,0:T(8,128)(2,1)S(1)} %add_convert_fusion.5), channel_id=1, source_target_pairs={{0,4},{1,3},{4,8},{5,1},{8,12},{9,5},{12,14},{13,9},{14,10},{15,13... | collective-permute-start | bytes 1572872 | tf_op jit(solution)/shard_map/ppermute | solution.py:223
  49.4 3.7 %shard_map.105 = (bf16[128,2048]{1,0:T(8,128)(2,1)S(1)}, bf16[128,2048]{1,0:T(8,128)(2,1)S(1)}) custom-call(s32[1]{0:T(128)} %bitcast.2.me_ref, bf16[2080,128]{1,0:T(8,128)(2,1)S(1)} %collective-permute-done.5.refs_0_, bf16[2080,128]{1,0:T(8,128)(2,1)S(1)} %collective-permute-done.15.refs_1_, bf16[2048,768]{1,0:T(8,128)(2,1)S(1)} %get-tuple-element.34.refs_2_, ...), custom_call_target="tpu_custom_call" | custom-call | flops 2717908992 | bytes 2097152 | tf_op jit(solution)/shard_map/pallas_call | solution.py:196
  55.3 3.1 %collective-permute-done.25 = bf16[128,2048]{1,0:T(8,128)(2,1)S(1)} collective-permute-done((bf16[128,2048]{1,0:T(8,128)(2,1)S(1)}, bf16[128,2048]{1,0:T(8,128)(2,1)S(1)}, u32[]{:S(2)}, u32[]{:S(2)}) %collective-permute-start.25) | collective-permute-done | bytes 524320 | tf_op jit(solution)/shard_map/ppermute | solution.py:223
  58.6 2.1 %collective-permute-start.26 = (bf16[128,2048]{1,0:T(8,128)(2,1)S(1)}, bf16[128,2048]{1,0:T(8,128)(2,1)S(1)}, u32[]{:S(2)}, u32[]{:S(2)}) collective-permute-start(bf16[128,2048]{1,0:T(8,128)(2,1)S(1)} %add_convert_fusion.4), channel_id=1, source_target_pairs={{0,4},{1,3},{4,8},{5,1},{8,12},{9,5},{12,14},{13,9},{14,10},{15,13... | collective-permute-start | bytes 1572872 | tf_op jit(solution)/shard_map/ppermute | solution.py:223
  60.8 3.7 %shard_map.104 = (bf16[128,2048]{1,0:T(8,128)(2,1)S(1)}, bf16[128,2048]{1,0:T(8,128)(2,1)S(1)}) custom-call(s32[1]{0:T(128)} %bitcast.2.me_ref, bf16[2080,128]{1,0:T(8,128)(2,1)S(1)} %collective-permute-done.6.refs_0_, bf16[2080,128]{1,0:T(8,128)(2,1)S(1)} %collective-permute-done.13.refs_1_, bf16[2048,768]{1,0:T(8,128)(2,1)S(1)} %get-tuple-element.34.refs_2_, ...), custom_call_target="tpu_custom_call" | custom-call | flops 2717908992 | bytes 2097152 | tf_op jit(solution)/shard_map/pallas_call | solution.py:196
  66.6 3.1 %collective-permute-done.26 = bf16[128,2048]{1,0:T(8,128)(2,1)S(1)} collective-permute-done((bf16[128,2048]{1,0:T(8,128)(2,1)S(1)}, bf16[128,2048]{1,0:T(8,128)(2,1)S(1)}, u32[]{:S(2)}, u32[]{:S(2)}) %collective-permute-start.26) | collective-permute-done | bytes 524320 | tf_op jit(solution)/shard_map/ppermute | solution.py:223
  70.0 2.3 %collective-permute-start.27 = (bf16[128,2048]{1,0:T(8,128)(2,1)S(1)}, bf16[128,2048]{1,0:T(8,128)(2,1)S(1)}, u32[]{:S(2)}, u32[]{:S(2)}) collective-permute-start(bf16[128,2048]{1,0:T(8,128)(2,1)S(1)} %add_convert_fusion.3), channel_id=1, source_target_pairs={{0,4},{1,3},{4,8},{5,1},{8,12},{9,5},{12,14},{13,9},{14,10},{15,13... | collective-permute-start | bytes 1572872 | tf_op jit(solution)/shard_map/ppermute | solution.py:223
  72.3 3.7 %shard_map.103 = (bf16[128,2048]{1,0:T(8,128)(2,1)S(1)}, bf16[128,2048]{1,0:T(8,128)(2,1)S(1)}) custom-call(s32[1]{0:T(128)} %bitcast.2.me_ref, bf16[2080,128]{1,0:T(8,128)(2,1)S(1)} %collective-permute-done.7.refs_0_, bf16[2080,128]{1,0:T(8,128)(2,1)S(1)} %collective-permute-done.11.refs_1_, bf16[2048,768]{1,0:T(8,128)(2,1)S(1)} %get-tuple-element.34.refs_2_, ...), custom_call_target="tpu_custom_call" | custom-call | flops 2717908992 | bytes 2097152 | tf_op jit(solution)/shard_map/pallas_call | solution.py:196
  76.6 4.4 %collective-permute-done.27 = bf16[128,2048]{1,0:T(8,128)(2,1)S(1)} collective-permute-done((bf16[128,2048]{1,0:T(8,128)(2,1)S(1)}, bf16[128,2048]{1,0:T(8,128)(2,1)S(1)}, u32[]{:S(2)}, u32[]{:S(2)}) %collective-permute-start.27) | collective-permute-done | bytes 524320 | tf_op jit(solution)/shard_map/ppermute | solution.py:223
  81.3 2.1 %collective-permute-start.28 = (bf16[128,2048]{1,0:T(8,128)(2,1)S(1)}, bf16[128,2048]{1,0:T(8,128)(2,1)S(1)}, u32[]{:S(2)}, u32[]{:S(2)}) collective-permute-start(bf16[128,2048]{1,0:T(8,128)(2,1)S(1)} %add_convert_fusion.2), channel_id=1, source_target_pairs={{0,4},{1,3},{4,8},{5,1},{8,12},{9,5},{12,14},{13,9},{14,10},{15,13... | collective-permute-start | bytes 1572872 | tf_op jit(solution)/shard_map/ppermute | solution.py:223
  83.4 3.7 %shard_map.102 = (bf16[128,2048]{1,0:T(8,128)(2,1)S(1)}, bf16[128,2048]{1,0:T(8,128)(2,1)S(1)}) custom-call(s32[1]{0:T(128)} %bitcast.2.me_ref, bf16[2080,128]{1,0:T(8,128)(2,1)S(1)} %collective-permute-done.8.refs_0_, bf16[2080,128]{1,0:T(8,128)(2,1)S(1)} %collective-permute-done.9.refs_1_, bf16[2048,768]{1,0:T(8,128)(2,1)S(1)} %get-tuple-element.34.refs_2_, ...), custom_call_target="tpu_custom_call" | custom-call | flops 2717908992 | bytes 2097152 | tf_op jit(solution)/shard_map/pallas_call | solution.py:196
  87.7 2.8 %collective-permute-done.28 = bf16[128,2048]{1,0:T(8,128)(2,1)S(1)} collective-permute-done((bf16[128,2048]{1,0:T(8,128)(2,1)S(1)}, bf16[128,2048]{1,0:T(8,128)(2,1)S(1)}, u32[]{:S(2)}, u32[]{:S(2)}) %collective-permute-start.28) | collective-permute-done | bytes 524320 | tf_op jit(solution)/shard_map/ppermute | solution.py:223
  90.8 2.1 %collective-permute-start.29 = (bf16[128,2048]{1,0:T(8,128)(2,1)S(1)}, bf16[128,2048]{1,0:T(8,128)(2,1)S(1)}, u32[]{:S(2)}, u32[]{:S(2)}) collective-permute-start(bf16[128,2048]{1,0:T(8,128)(2,1)S(1)} %add_convert_fusion.1), channel_id=1, source_target_pairs={{0,4},{1,3},{4,8},{5,1},{8,12},{9,5},{12,14},{13,9},{14,10},{15,13... | collective-permute-start | bytes 1572872 | tf_op jit(solution)/shard_map/ppermute | solution.py:223
  92.9 7.1 %collective-permute-done.29 = bf16[128,2048]{1,0:T(8,128)(2,1)S(1)} collective-permute-done((bf16[128,2048]{1,0:T(8,128)(2,1)S(1)}, bf16[128,2048]{1,0:T(8,128)(2,1)S(1)}, u32[]{:S(2)}, u32[]{:S(2)}) %collective-permute-start.29) | collective-permute-done | bytes 524320 | tf_op jit(solution)/shard_map/ppermute | solution.py:223
  (53 shorter events, 20.2 us)
Async XLA Ops:
  1.7 9.8 %collective-permute-start = (bf16[2080,128]{1,0:T(8,128)(2,1)S(1)}, bf16[2080,128]{1,0:T(8,128)(2,1)S(1)}, u32[]{:S(2)}, u32[]{:S(2)}) collective-permute-start(bf16[2080,128]{1,0:T(8,128)(2,1)S(1)} %shard_map.100.refs_0_), channel_id=1, source_target_pairs={{0,4},{1,3},{4,8},{5,1},{8,12},{9,5},{12,14},{13,9},{14,10},{15,13... | collective-permute-start | bytes 1597448 | tf_op jit(solution)/shard_map/ppermute | solution.py:223
  11.6 9.3 %collective-permute-start.3 = (bf16[2080,128]{1,0:T(8,128)(2,1)S(1)}, bf16[2080,128]{1,0:T(8,128)(2,1)S(1)}, u32[]{:S(2)}, u32[]{:S(2)}) collective-permute-start(bf16[2080,128]{1,0:T(8,128)(2,1)S(1)} %collective-permute-done.refs_0_), channel_id=1, source_target_pairs={{0,4},{1,3},{4,8},{5,1},{8,12},{9,5},{12,14},{13,9},{14,10},{15,13... | collective-permute-start | bytes 1597448 | tf_op jit(solution)/shard_map/ppermute | solution.py:223
  17.4 5.5 %collective-permute-start.22 = (bf16[128,2048]{1,0:T(8,128)(2,1)S(1)}, bf16[128,2048]{1,0:T(8,128)(2,1)S(1)}, u32[]{:S(2)}, u32[]{:S(2)}) collective-permute-start(bf16[128,2048]{1,0:T(8,128)(2,1)S(1)} %get-tuple-element.52), channel_id=1, source_target_pairs={{0,1},{1,0},{2,3},{3,2},{4,5},{5,4},{6,7},{7,6},{8,9},{9,8},{10,11... | collective-permute-start | bytes 1572872 | tf_op jit(solution)/shard_map/ppermute | solution.py:220
  20.8 9.3 %collective-permute-start.4 = (bf16[2080,128]{1,0:T(8,128)(2,1)S(1)}, bf16[2080,128]{1,0:T(8,128)(2,1)S(1)}, u32[]{:S(2)}, u32[]{:S(2)}) collective-permute-start(bf16[2080,128]{1,0:T(8,128)(2,1)S(1)} %collective-permute-done.3.refs_0_), channel_id=1, source_target_pairs={{0,4},{1,3},{4,8},{5,1},{8,12},{9,5},{12,14},{13,9},{14,10},{15,13... | collective-permute-start | bytes 1597448 | tf_op jit(solution)/shard_map/ppermute | solution.py:223
  23.1 12.7 %collective-permute-start.23 = (bf16[128,2048]{1,0:T(8,128)(2,1)S(1)}, bf16[128,2048]{1,0:T(8,128)(2,1)S(1)}, u32[]{:S(2)}, u32[]{:S(2)}) collective-permute-start(bf16[128,2048]{1,0:T(8,128)(2,1)S(1)} %add_convert_fusion.7), channel_id=1, source_target_pairs={{0,4},{1,3},{4,8},{5,1},{8,12},{9,5},{12,14},{13,9},{14,10},{15,13... | collective-permute-start | bytes 1572872 | tf_op jit(solution)/shard_map/ppermute | solution.py:223
  28.4 7.3 %collective-permute-start.20 = (bf16[128,2048]{1,0:T(8,128)(2,1)S(1)}, bf16[128,2048]{1,0:T(8,128)(2,1)S(1)}, u32[]{:S(2)}, u32[]{:S(2)}) collective-permute-start(bf16[128,2048]{1,0:T(8,128)(2,1)S(1)} %get-tuple-element.50), channel_id=1, source_target_pairs={{0,1},{1,0},{2,3},{3,2},{4,5},{5,4},{6,7},{7,6},{8,9},{9,8},{10,11... | collective-permute-start | bytes 1572872 | tf_op jit(solution)/shard_map/ppermute | solution.py:220
  30.1 8.2 %collective-permute-start.17 = (bf16[2080,128]{1,0:T(8,128)(2,1)S(1)}, bf16[2080,128]{1,0:T(8,128)(2,1)S(1)}, u32[]{:S(2)}, u32[]{:S(2)}) collective-permute-start(bf16[2080,128]{1,0:T(8,128)(2,1)S(1)} %collective-permute-done.4.refs_0_), channel_id=1, source_target_pairs={{0,1},{1,0},{2,3},{3,2},{4,5},{5,4},{6,7},{7,6},{8,9},{9,8},{10,11... | collective-permute-start | bytes 1597448 | tf_op jit(solution)/shard_map/ppermute | solution.py:220
  30.1 12.0 %collective-permute-start.5 = (bf16[2080,128]{1,0:T(8,128)(2,1)S(1)}, bf16[2080,128]{1,0:T(8,128)(2,1)S(1)}, u32[]{:S(2)}, u32[]{:S(2)}) collective-permute-start(bf16[2080,128]{1,0:T(8,128)(2,1)S(1)} %collective-permute-done.4.refs_0_), channel_id=1, source_target_pairs={{0,4},{1,3},{4,8},{5,1},{8,12},{9,5},{12,14},{13,9},{14,10},{15,13... | collective-permute-start | bytes 1597448 | tf_op jit(solution)/shard_map/ppermute | solution.py:223
  36.0 11.1 %collective-permute-start.24 = (bf16[128,2048]{1,0:T(8,128)(2,1)S(1)}, bf16[128,2048]{1,0:T(8,128)(2,1)S(1)}, u32[]{:S(2)}, u32[]{:S(2)}) collective-permute-start(bf16[128,2048]{1,0:T(8,128)(2,1)S(1)} %add_convert_fusion.6), channel_id=1, source_target_pairs={{0,4},{1,3},{4,8},{5,1},{8,12},{9,5},{12,14},{13,9},{14,10},{15,13... | collective-permute-start | bytes 1572872 | tf_op jit(solution)/shard_map/ppermute | solution.py:223
  42.1 7.3 %collective-permute-start.15 = (bf16[2080,128]{1,0:T(8,128)(2,1)S(1)}, bf16[2080,128]{1,0:T(8,128)(2,1)S(1)}, u32[]{:S(2)}, u32[]{:S(2)}) collective-permute-start(bf16[2080,128]{1,0:T(8,128)(2,1)S(1)} %collective-permute-done.5.refs_0_), channel_id=1, source_target_pairs={{0,1},{1,0},{2,3},{3,2},{4,5},{5,4},{6,7},{7,6},{8,9},{9,8},{10,11... | collective-permute-start | bytes 1597448 | tf_op jit(solution)/shard_map/ppermute | solution.py:220
  42.6 10.6 %collective-permute-start.6 = (bf16[2080,128]{1,0:T(8,128)(2,1)S(1)}, bf16[2080,128]{1,0:T(8,128)(2,1)S(1)}, u32[]{:S(2)}, u32[]{:S(2)}) collective-permute-start(bf16[2080,128]{1,0:T(8,128)(2,1)S(1)} %collective-permute-done.5.refs_0_), channel_id=1, source_target_pairs={{0,4},{1,3},{4,8},{5,1},{8,12},{9,5},{12,14},{13,9},{14,10},{15,13... | collective-permute-start | bytes 1597448 | tf_op jit(solution)/shard_map/ppermute | solution.py:223
  47.3 11.1 %collective-permute-start.25 = (bf16[128,2048]{1,0:T(8,128)(2,1)S(1)}, bf16[128,2048]{1,0:T(8,128)(2,1)S(1)}, u32[]{:S(2)}, u32[]{:S(2)}) collective-permute-start(bf16[128,2048]{1,0:T(8,128)(2,1)S(1)} %add_convert_fusion.5), channel_id=1, source_target_pairs={{0,4},{1,3},{4,8},{5,1},{8,12},{9,5},{12,14},{13,9},{14,10},{15,13... | collective-permute-start | bytes 1572872 | tf_op jit(solution)/shard_map/ppermute | solution.py:223
  53.2 5.2 %collective-permute-start.16 = (bf16[128,2048]{1,0:T(8,128)(2,1)S(1)}, bf16[128,2048]{1,0:T(8,128)(2,1)S(1)}, u32[]{:S(2)}, u32[]{:S(2)}) collective-permute-start(bf16[128,2048]{1,0:T(8,128)(2,1)S(1)} %get-tuple-element.46), channel_id=1, source_target_pairs={{0,1},{1,0},{2,3},{3,2},{4,5},{5,4},{6,7},{7,6},{8,9},{9,8},{10,11... | collective-permute-start | bytes 1572872 | tf_op jit(solution)/shard_map/ppermute | solution.py:220
  53.2 7.5 %collective-permute-start.13 = (bf16[2080,128]{1,0:T(8,128)(2,1)S(1)}, bf16[2080,128]{1,0:T(8,128)(2,1)S(1)}, u32[]{:S(2)}, u32[]{:S(2)}) collective-permute-start(bf16[2080,128]{1,0:T(8,128)(2,1)S(1)} %collective-permute-done.6.refs_0_), channel_id=1, source_target_pairs={{0,1},{1,0},{2,3},{3,2},{4,5},{5,4},{6,7},{7,6},{8,9},{9,8},{10,11... | collective-permute-start | bytes 1597448 | tf_op jit(solution)/shard_map/ppermute | solution.py:220
  53.7 10.8 %collective-permute-start.7 = (bf16[2080,128]{1,0:T(8,128)(2,1)S(1)}, bf16[2080,128]{1,0:T(8,128)(2,1)S(1)}, u32[]{:S(2)}, u32[]{:S(2)}) collective-permute-start(bf16[2080,128]{1,0:T(8,128)(2,1)S(1)} %collective-permute-done.6.refs_0_), channel_id=1, source_target_pairs={{0,4},{1,3},{4,8},{5,1},{8,12},{9,5},{12,14},{13,9},{14,10},{15,13... | collective-permute-start | bytes 1597448 | tf_op jit(solution)/shard_map/ppermute | solution.py:223
  58.6 11.1 %collective-permute-start.26 = (bf16[128,2048]{1,0:T(8,128)(2,1)S(1)}, bf16[128,2048]{1,0:T(8,128)(2,1)S(1)}, u32[]{:S(2)}, u32[]{:S(2)}) collective-permute-start(bf16[128,2048]{1,0:T(8,128)(2,1)S(1)} %add_convert_fusion.4), channel_id=1, source_target_pairs={{0,4},{1,3},{4,8},{5,1},{8,12},{9,5},{12,14},{13,9},{14,10},{15,13... | collective-permute-start | bytes 1572872 | tf_op jit(solution)/shard_map/ppermute | solution.py:223
  64.5 5.2 %collective-permute-start.14 = (bf16[128,2048]{1,0:T(8,128)(2,1)S(1)}, bf16[128,2048]{1,0:T(8,128)(2,1)S(1)}, u32[]{:S(2)}, u32[]{:S(2)}) collective-permute-start(bf16[128,2048]{1,0:T(8,128)(2,1)S(1)} %get-tuple-element.44), channel_id=1, source_target_pairs={{0,1},{1,0},{2,3},{3,2},{4,5},{5,4},{6,7},{7,6},{8,9},{9,8},{10,11... | collective-permute-start | bytes 1572872 | tf_op jit(solution)/shard_map/ppermute | solution.py:220
  64.6 7.7 %collective-permute-start.11 = (bf16[2080,128]{1,0:T(8,128)(2,1)S(1)}, bf16[2080,128]{1,0:T(8,128)(2,1)S(1)}, u32[]{:S(2)}, u32[]{:S(2)}) collective-permute-start(bf16[2080,128]{1,0:T(8,128)(2,1)S(1)} %collective-permute-done.7.refs_0_), channel_id=1, source_target_pairs={{0,1},{1,0},{2,3},{3,2},{4,5},{5,4},{6,7},{7,6},{8,9},{9,8},{10,11... | collective-permute-start | bytes 1597448 | tf_op jit(solution)/shard_map/ppermute | solution.py:220
  65.1 11.0 %collective-permute-start.8 = (bf16[2080,128]{1,0:T(8,128)(2,1)S(1)}, bf16[2080,128]{1,0:T(8,128)(2,1)S(1)}, u32[]{:S(2)}, u32[]{:S(2)}) collective-permute-start(bf16[2080,128]{1,0:T(8,128)(2,1)S(1)} %collective-permute-done.7.refs_0_), channel_id=1, source_target_pairs={{0,4},{1,3},{4,8},{5,1},{8,12},{9,5},{12,14},{13,9},{14,10},{15,13... | collective-permute-start | bytes 1597448 | tf_op jit(solution)/shard_map/ppermute | solution.py:223
  70.0 11.1 %collective-permute-start.27 = (bf16[128,2048]{1,0:T(8,128)(2,1)S(1)}, bf16[128,2048]{1,0:T(8,128)(2,1)S(1)}, u32[]{:S(2)}, u32[]{:S(2)}) collective-permute-start(bf16[128,2048]{1,0:T(8,128)(2,1)S(1)} %add_convert_fusion.3), channel_id=1, source_target_pairs={{0,4},{1,3},{4,8},{5,1},{8,12},{9,5},{12,14},{13,9},{14,10},{15,13... | collective-permute-start | bytes 1572872 | tf_op jit(solution)/shard_map/ppermute | solution.py:223
  76.1 7.3 %collective-permute-start.9 = (bf16[2080,128]{1,0:T(8,128)(2,1)S(1)}, bf16[2080,128]{1,0:T(8,128)(2,1)S(1)}, u32[]{:S(2)}, u32[]{:S(2)}) collective-permute-start(bf16[2080,128]{1,0:T(8,128)(2,1)S(1)} %collective-permute-done.8.refs_0_), channel_id=1, source_target_pairs={{0,1},{1,0},{2,3},{3,2},{4,5},{5,4},{6,7},{7,6},{8,9},{9,8},{10,11... | collective-permute-start | bytes 1597448 | tf_op jit(solution)/shard_map/ppermute | solution.py:220
  81.3 9.2 %collective-permute-start.28 = (bf16[128,2048]{1,0:T(8,128)(2,1)S(1)}, bf16[128,2048]{1,0:T(8,128)(2,1)S(1)}, u32[]{:S(2)}, u32[]{:S(2)}) collective-permute-start(bf16[128,2048]{1,0:T(8,128)(2,1)S(1)} %add_convert_fusion.2), channel_id=1, source_target_pairs={{0,4},{1,3},{4,8},{5,1},{8,12},{9,5},{12,14},{13,9},{14,10},{15,13... | collective-permute-start | bytes 1572872 | tf_op jit(solution)/shard_map/ppermute | solution.py:223
  87.2 5.7 %collective-permute-start.2 = (bf16[128,2048]{1,0:T(8,128)(2,1)S(1)}, bf16[128,2048]{1,0:T(8,128)(2,1)S(1)}, u32[]{:S(2)}, u32[]{:S(2)}) collective-permute-start(bf16[128,2048]{1,0:T(8,128)(2,1)S(1)} %get-tuple-element.32), channel_id=1, source_target_pairs={{0,1},{1,0},{2,3},{3,2},{4,5},{5,4},{6,7},{7,6},{8,9},{9,8},{10,11... | collective-permute-start | bytes 1572872 | tf_op jit(solution)/shard_map/ppermute | solution.py:220
  90.8 9.2 %collective-permute-start.29 = (bf16[128,2048]{1,0:T(8,128)(2,1)S(1)}, bf16[128,2048]{1,0:T(8,128)(2,1)S(1)}, u32[]{:S(2)}, u32[]{:S(2)}) collective-permute-start(bf16[128,2048]{1,0:T(8,128)(2,1)S(1)} %add_convert_fusion.1), channel_id=1, source_target_pairs={{0,4},{1,3},{4,8},{5,1},{8,12},{9,5},{12,14},{13,9},{14,10},{15,13... | collective-permute-start | bytes 1572872 | tf_op jit(solution)/shard_map/ppermute | solution.py:223
  (6 other events, 22.5 us)

commit v3 on v2

--- a/solution.py
+++ b/solution.py
@@ -8,6 +8,7 @@
 from jax.sharding import PartitionSpec as P
 
 LANES = 128
+SPLIT = 1
 
 
 def ring_tables(devices):
@@ -230,19 +231,50 @@
 
     own = work(me, rows, swap(rows), weights, slots, hots, bring=True)
     own, weights = own[:2], own[2:]
-    coming = None
+    coming, total = None, None
     mine = rows
     for step in range(1, chips):
         mine = onward(mine)
         if step == 1:
             mine, own = lax.optimization_barrier((mine, own))
+        if total is not None:
+            me, total = lax.optimization_barrier((me, total))
+            coming = onward(total)
+            total = None
         kept, given = work(me, mine, swap(mine), weights, slots, hots)
+        if step >= chips - SPLIT:
+            taken = swap(given)
+            parts = coming if isinstance(coming, list) else [coming] * 2
+            coming = [onward(add_half(kept, taken, before, half)) for half, before in enumerate(parts)]
+            continue
         total = kept.astype(jnp.float32) + swap(given).astype(jnp.float32)
         if coming is not None:
             total = total + coming.astype(jnp.float32)
-        coming = onward(total.astype(jnp.bfloat16))
-    total = own[0].astype(jnp.float32) + swap(own[1]).astype(jnp.float32) + coming.astype(jnp.float32)
-    return total.astype(jnp.bfloat16).reshape(micros, held, width)
+        total = total.astype(jnp.bfloat16)
+    taken = swap(own[1])
+    halves = [add_half(own[0], taken, before, half) for half, before in enumerate(coming)]
+    return jnp.concatenate(halves).reshape(micros, held, width)
+
+
+def add_body(kept, taken, before, out, *, half):
+    size = out.shape[0]
+    cut = slice(half * size, (half + 1) * size)
+    came = cut if before.shape[0] > size else slice(None)
+    total = kept[cut].astype(jnp.float32) + taken[cut].astype(jnp.float32) + before[came].astype(jnp.float32)
+    out[...] = total.astype(out.dtype)
+
+
+def add_half(kept, taken, before, half):
+    size, width = kept.shape[0] // 2, kept.shape[1]
+    near = pl.BlockSpec(memory_space=pltpu.VMEM)
+    return pl.pallas_call(
+        functools.partial(add_body, half=half),
+        in_specs=[near] * 3,
+        out_specs=near,
+        out_shape=jax.ShapeDtypeStruct((size, width), kept.dtype),
+        compiler_params=pltpu.CompilerParams(vmem_limit_bytes=8 << 20),
+        cost_estimate=pl.CostEstimate(flops=0, bytes_accessed=(16 if half == 0 else 2) * size * width, transcendentals=0),
+    )(kept, taken, before)
 
 
 def solution(mesh):

time: 101 us -> 101 us (level)
  waiting for transfers between devices: 32.3 us -> 30.5 us
  starting transfers between devices: 32 us -> 33.7 us
    ppermute x14 -> x15, waiting for transfers between devices: 32.3 us -> 30.4 us  [onward(): return lax.ppermute(x, 'expert', around)]
    ppermute x14 -> x15, starting transfers between devices: 28.4 us -> 30 us  [onward(): return lax.ppermute(x, 'expert', around)]
    convert_element_type x8 -> x6, other arithmetic: 2.61 us -> 1.33 us  [shards(): total = total.astype(jnp.bfloat16)]
  transfers between devices with their start and end apart: 30 -> 31, of which waited for: 10 -> 11; matrix products, arithmetic and copies ran while one was open for 2% -> 1% of each run, Pallas kernels for 32% -> 33%
where the time goes in v3:
time: 101 us
  Pallas kernels  34.2 us (34%)
  starting transfers between devices  33.7 us (33%)
  waiting for transfers between devices  30.5 us (30%)
  other arithmetic  2.18 us (2%)
    pallas_call x8, Pallas kernels, work(): pl.pallas_call(body, in_specs=[pl.BlockSpec(memory_space=pltpu.SMEM)] + [...  32.6 us
    ppermute x15, waiting for transfers between devices, onward(): return lax.ppermute(x, 'expert', around)  30.4 us
    ppermute x15, starting transfers between devices, onward(): return lax.ppermute(x, 'expert', around)  30 us
    ppermute x16, starting transfers between devices, swap(): return lax.ppermute(x, 'expert', across)  3.64 us
  transfers between devices with their start and end apart: 31, of which 11 were waited for; matrix products, arithmetic and copies ran while one was open for 1% of the time, Pallas kernels for 33%

profile of v3, /device:TPU:0, one launch (start us, length us, event | category | flops | bytes accessed | tf_op | source)
XLA Modules:
  0.0 100.8 jit_solution(7471430191938710991)
XLA Ops:
  1.7 2.6 %collective-permute-start = (bf16[2080,128]{1,0:T(8,128)(2,1)S(1)}, bf16[2080,128]{1,0:T(8,128)(2,1)S(1)}, u32[]{:S(2)}, u32[]{:S(2)}) collective-permute-start(bf16[2080,128]{1,0:T(8,128)(2,1)S(1)} %shard_map.100.refs_0_), channel_id=1, source_target_pairs={{0,4},{1,3},{4,8},{5,1},{8,12},{9,5},{12,14},{13,9},{14,10},{15,13... | collective-permute-start | bytes 1597448 | tf_op jit(solution)/shard_map/ppermute | solution.py:224
  4.4 6.6 %shard_map.101 = (bf16[128,2048]{1,0:T(8,128)(2,1)S(1)}, bf16[128,2048]{1,0:T(8,128)(2,1)S(1)}, bf16[2048,768]{1,0:T(8,128)(2,1)S(1)}, bf16[2048,768]{1,0:T(8,12...) custom-call(s32[1]{0:T(128)} %bitcast.2.me_ref, ...), custom_call_target="tpu_custom_call" | custom-call | flops 2717908992 | bytes 2097152 | tf_op jit(solution)/shard_map/pallas_call | solution.py:197
  13.7 3.7 %shard_map.102 = (bf16[128,2048]{1,0:T(8,128)(2,1)S(1)}, bf16[128,2048]{1,0:T(8,128)(2,1)S(1)}) custom-call(s32[1]{0:T(128)} %bitcast.2.me_ref, bf16[2080,128]{1,0:T(8,128)(2,1)S(1)} %collective-permute-done.refs_0_, bf16[2080,128]{1,0:T(8,128)(2,1)S(1)} %collective-permute-done.3.refs_1_, bf16[2048,768]{1,0:T(8,128)(2,1)S(1)} %get-tuple-element.46.refs_2_, ...), custom_call_target="tpu_custom_call" | custom-call | flops 2717908992 | bytes 2097152 | tf_op jit(solution)/shard_map/pallas_call | solution.py:197
  17.6 3.2 %collective-permute-done.5.refs_0_ = bf16[2080,128]{1,0:T(8,128)(2,1)S(1)} collective-permute-done((bf16[2080,128]{1,0:T(8,128)(2,1)S(1)}, bf16[2080,128]{1,0:T(8,128)(2,1)S(1)}, u32[]{:S(2)}, u32[]{:S(2)}) %collective-permute-start.5) | collective-permute-done | bytes 532512 | tf_op jit(solution)/shard_map/ppermute | solution.py:224
  24.7 3.7 %shard_map.103 = (bf16[128,2048]{1,0:T(8,128)(2,1)S(1)}, bf16[128,2048]{1,0:T(8,128)(2,1)S(1)}) custom-call(s32[1]{0:T(128)} %bitcast.2.me_ref, bf16[2080,128]{1,0:T(8,128)(2,1)S(1)} %collective-permute-done.5.refs_0_, bf16[2080,128]{1,0:T(8,128)(2,1)S(1)} %collective-permute-done.6.refs_1_, bf16[2048,768]{1,0:T(8,128)(2,1)S(1)} %get-tuple-element.46.refs_2_, ...), custom_call_target="tpu_custom_call" | custom-call | flops 2717908992 | bytes 2097152 | tf_op jit(solution)/shard_map/pallas_call | solution.py:197
  32.2 3.5 %collective-permute-done.8 = bf16[128,2048]{1,0:T(8,128)(2,1)S(1)} collective-permute-done((bf16[128,2048]{1,0:T(8,128)(2,1)S(1)}, bf16[128,2048]{1,0:T(8,128)(2,1)S(1)}, u32[]{:S(2)}, u32[]{:S(2)}) %collective-permute-start.8) | collective-permute-done | bytes 524320 | tf_op jit(solution)/shard_map/ppermute | solution.py:224
  36.0 2.3 %collective-permute-start.12 = (bf16[128,2048]{1,0:T(8,128)(2,1)S(1)}, bf16[128,2048]{1,0:T(8,128)(2,1)S(1)}, u32[]{:S(2)}, u32[]{:S(2)}) collective-permute-start(bf16[128,2048]{1,0:T(8,128)(2,1)S(1)} %add_convert_fusion.4), channel_id=1, source_target_pairs={{0,4},{1,3},{4,8},{5,1},{8,12},{9,5},{12,14},{13,9},{14,10},{15,13... | collective-permute-start | bytes 1572872 | tf_op jit(solution)/shard_map/ppermute | solution.py:224
  38.3 3.7 %shard_map.104 = (bf16[128,2048]{1,0:T(8,128)(2,1)S(1)}, bf16[128,2048]{1,0:T(8,128)(2,1)S(1)}) custom-call(s32[1]{0:T(128)} %bitcast.2.me_ref, bf16[2080,128]{1,0:T(8,128)(2,1)S(1)} %collective-permute-done.9.refs_0_, bf16[2080,128]{1,0:T(8,128)(2,1)S(1)} %collective-permute-done.10.refs_1_, bf16[2048,768]{1,0:T(8,128)(2,1)S(1)} %get-tuple-element.46.refs_2_, ...), custom_call_target="tpu_custom_call" | custom-call | flops 2717908992 | bytes 2097152 | tf_op jit(solution)/shard_map/pallas_call | solution.py:197
  44.2 2.9 %collective-permute-done.12 = bf16[128,2048]{1,0:T(8,128)(2,1)S(1)} collective-permute-done((bf16[128,2048]{1,0:T(8,128)(2,1)S(1)}, bf16[128,2048]{1,0:T(8,128)(2,1)S(1)}, u32[]{:S(2)}, u32[]{:S(2)}) %collective-permute-start.12) | collective-permute-done | bytes 524320 | tf_op jit(solution)/shard_map/ppermute | solution.py:224
  47.3 2.1 %collective-permute-start.16 = (bf16[128,2048]{1,0:T(8,128)(2,1)S(1)}, bf16[128,2048]{1,0:T(8,128)(2,1)S(1)}, u32[]{:S(2)}, u32[]{:S(2)}) collective-permute-start(bf16[128,2048]{1,0:T(8,128)(2,1)S(1)} %add_convert_fusion.3), channel_id=1, source_target_pairs={{0,4},{1,3},{4,8},{5,1},{8,12},{9,5},{12,14},{13,9},{14,10},{15,13... | collective-permute-start | bytes 1572872 | tf_op jit(solution)/shard_map/ppermute | solution.py:224
  49.4 3.7 %shard_map.105 = (bf16[128,2048]{1,0:T(8,128)(2,1)S(1)}, bf16[128,2048]{1,0:T(8,128)(2,1)S(1)}) custom-call(s32[1]{0:T(128)} %bitcast.2.me_ref, bf16[2080,128]{1,0:T(8,128)(2,1)S(1)} %collective-permute-done.13.refs_0_, bf16[2080,128]{1,0:T(8,128)(2,1)S(1)} %collective-permute-done.14.refs_1_, bf16[2048,768]{1,0:T(8,128)(2,1)S(1)} %get-tuple-element.46.refs_2_, ...), custom_call_target="tpu_custom_call" | custom-call | flops 2717908992 | bytes 2097152 | tf_op jit(solution)/shard_map/pallas_call | solution.py:197
  55.3 3.1 %collective-permute-done.16 = bf16[128,2048]{1,0:T(8,128)(2,1)S(1)} collective-permute-done((bf16[128,2048]{1,0:T(8,128)(2,1)S(1)}, bf16[128,2048]{1,0:T(8,128)(2,1)S(1)}, u32[]{:S(2)}, u32[]{:S(2)}) %collective-permute-start.16) | collective-permute-done | bytes 524320 | tf_op jit(solution)/shard_map/ppermute | solution.py:224
  58.6 2.1 %collective-permute-start.20 = (bf16[128,2048]{1,0:T(8,128)(2,1)S(1)}, bf16[128,2048]{1,0:T(8,128)(2,1)S(1)}, u32[]{:S(2)}, u32[]{:S(2)}) collective-permute-start(bf16[128,2048]{1,0:T(8,128)(2,1)S(1)} %add_convert_fusion.2), channel_id=1, source_target_pairs={{0,4},{1,3},{4,8},{5,1},{8,12},{9,5},{12,14},{13,9},{14,10},{15,13... | collective-permute-start | bytes 1572872 | tf_op jit(solution)/shard_map/ppermute | solution.py:224
  60.8 3.7 %shard_map.106 = (bf16[128,2048]{1,0:T(8,128)(2,1)S(1)}, bf16[128,2048]{1,0:T(8,128)(2,1)S(1)}) custom-call(s32[1]{0:T(128)} %bitcast.2.me_ref, bf16[2080,128]{1,0:T(8,128)(2,1)S(1)} %collective-permute-done.17.refs_0_, bf16[2080,128]{1,0:T(8,128)(2,1)S(1)} %collective-permute-done.18.refs_1_, bf16[2048,768]{1,0:T(8,128)(2,1)S(1)} %get-tuple-element.46.refs_2_, ...), custom_call_target="tpu_custom_call" | custom-call | flops 2717908992 | bytes 2097152 | tf_op jit(solution)/shard_map/pallas_call | solution.py:197
  66.6 3.1 %collective-permute-done.20 = bf16[128,2048]{1,0:T(8,128)(2,1)S(1)} collective-permute-done((bf16[128,2048]{1,0:T(8,128)(2,1)S(1)}, bf16[128,2048]{1,0:T(8,128)(2,1)S(1)}, u32[]{:S(2)}, u32[]{:S(2)}) %collective-permute-start.20) | collective-permute-done | bytes 524320 | tf_op jit(solution)/shard_map/ppermute | solution.py:224
  70.0 2.3 %collective-permute-start.24 = (bf16[128,2048]{1,0:T(8,128)(2,1)S(1)}, bf16[128,2048]{1,0:T(8,128)(2,1)S(1)}, u32[]{:S(2)}, u32[]{:S(2)}) collective-permute-start(bf16[128,2048]{1,0:T(8,128)(2,1)S(1)} %add_convert_fusion.1), channel_id=1, source_target_pairs={{0,4},{1,3},{4,8},{5,1},{8,12},{9,5},{12,14},{13,9},{14,10},{15,13... | collective-permute-start | bytes 1572872 | tf_op jit(solution)/shard_map/ppermute | solution.py:224
  72.3 3.7 %shard_map.107 = (bf16[128,2048]{1,0:T(8,128)(2,1)S(1)}, bf16[128,2048]{1,0:T(8,128)(2,1)S(1)}) custom-call(s32[1]{0:T(128)} %bitcast.2.me_ref, bf16[2080,128]{1,0:T(8,128)(2,1)S(1)} %collective-permute-done.21.refs_0_, bf16[2080,128]{1,0:T(8,128)(2,1)S(1)} %collective-permute-done.22.refs_1_, bf16[2048,768]{1,0:T(8,128)(2,1)S(1)} %get-tuple-element.46.refs_2_, ...), custom_call_target="tpu_custom_call" | custom-call | flops 2717908992 | bytes 2097152 | tf_op jit(solution)/shard_map/pallas_call | solution.py:197
  76.6 4.4 %collective-permute-done.24 = bf16[128,2048]{1,0:T(8,128)(2,1)S(1)} collective-permute-done((bf16[128,2048]{1,0:T(8,128)(2,1)S(1)}, bf16[128,2048]{1,0:T(8,128)(2,1)S(1)}, u32[]{:S(2)}, u32[]{:S(2)}) %collective-permute-start.24) | collective-permute-done | bytes 524320 | tf_op jit(solution)/shard_map/ppermute | solution.py:224
  81.3 2.1 %collective-permute-start.28 = (bf16[128,2048]{1,0:T(8,128)(2,1)S(1)}, bf16[128,2048]{1,0:T(8,128)(2,1)S(1)}, u32[]{:S(2)}, u32[]{:S(2)}) collective-permute-start(bf16[128,2048]{1,0:T(8,128)(2,1)S(1)} %add_convert_fusion), channel_id=1, source_target_pairs={{0,4},{1,3},{4,8},{5,1},{8,12},{9,5},{12,14},{13,9},{14,10},{15,13... | collective-permute-start | bytes 1572872 | tf_op jit(solution)/shard_map/ppermute | solution.py:224
  83.4 3.7 %shard_map.108 = (bf16[128,2048]{1,0:T(8,128)(2,1)S(1)}, bf16[128,2048]{1,0:T(8,128)(2,1)S(1)}) custom-call(s32[1]{0:T(128)} %bitcast.2.me_ref, bf16[2080,128]{1,0:T(8,128)(2,1)S(1)} %collective-permute-done.25.refs_0_, bf16[2080,128]{1,0:T(8,128)(2,1)S(1)} %collective-permute-done.26.refs_1_, bf16[2048,768]{1,0:T(8,128)(2,1)S(1)} %get-tuple-element.46.refs_2_, ...), custom_call_target="tpu_custom_call" | custom-call | flops 2717908992 | bytes 2097152 | tf_op jit(solution)/shard_map/pallas_call | solution.py:197
  87.7 2.8 %collective-permute-done.28.before = bf16[128,2048]{1,0:T(8,128)(2,1)S(1)} collective-permute-done((bf16[128,2048]{1,0:T(8,128)(2,1)S(1)}, bf16[128,2048]{1,0:T(8,128)(2,1)S(1)}, u32[]{:S(2)}, u32[]{:S(2)}) %collective-permute-start.28) | collective-permute-done | bytes 524320 | tf_op jit(solution)/shard_map/ppermute | solution.py:224
  90.6 2.1 %collective-permute-start.30 = (bf16[64,2048]{1,0:T(8,128)(2,1)S(1)}, bf16[64,2048]{1,0:T(8,128)(2,1)S(1)}, u32[]{:S(2)}, u32[]{:S(2)}) collective-permute-start(bf16[64,2048]{1,0:T(8,128)(2,1)S(1)} %shard_map.111), channel_id=1, source_target_pairs={{0,4},{1,3},{4,8},{5,1},{8,12},{9,5},{12,14},{13,9},{14,10},{15,13... | collective-permute-start | bytes 786440 | tf_op jit(solution)/shard_map/ppermute | solution.py:224
  94.5 2.6 %collective-permute-done.30.before = bf16[64,2048]{1,0:T(8,128)(2,1)S(1)} collective-permute-done((bf16[64,2048]{1,0:T(8,128)(2,1)S(1)}, bf16[64,2048]{1,0:T(8,128)(2,1)S(1)}, u32[]{:S(2)}, u32[]{:S(2)}) %collective-permute-start.30) | collective-permute-done | bytes 262176 | tf_op jit(solution)/shard_map/ppermute | solution.py:224
  97.1 2.7 %collective-permute-done.29.before = bf16[64,2048]{1,0:T(8,128)(2,1)S(1)} collective-permute-done((bf16[64,2048]{1,0:T(8,128)(2,1)S(1)}, bf16[64,2048]{1,0:T(8,128)(2,1)S(1)}, u32[]{:S(2)}, u32[]{:S(2)}) %collective-permute-start.29) | collective-permute-done | bytes 262176 | tf_op jit(solution)/shard_map/ppermute | solution.py:224
  (58 shorter events, 23.9 us)
Async XLA Ops:
  1.7 9.8 %collective-permute-start = (bf16[2080,128]{1,0:T(8,128)(2,1)S(1)}, bf16[2080,128]{1,0:T(8,128)(2,1)S(1)}, u32[]{:S(2)}, u32[]{:S(2)}) collective-permute-start(bf16[2080,128]{1,0:T(8,128)(2,1)S(1)} %shard_map.100.refs_0_), channel_id=1, source_target_pairs={{0,4},{1,3},{4,8},{5,1},{8,12},{9,5},{12,14},{13,9},{14,10},{15,13... | collective-permute-start | bytes 1597448 | tf_op jit(solution)/shard_map/ppermute | solution.py:224
  11.6 9.3 %collective-permute-start.5 = (bf16[2080,128]{1,0:T(8,128)(2,1)S(1)}, bf16[2080,128]{1,0:T(8,128)(2,1)S(1)}, u32[]{:S(2)}, u32[]{:S(2)}) collective-permute-start(bf16[2080,128]{1,0:T(8,128)(2,1)S(1)} %collective-permute-done.refs_0_), channel_id=1, source_target_pairs={{0,4},{1,3},{4,8},{5,1},{8,12},{9,5},{12,14},{13,9},{14,10},{15,13... | collective-permute-start | bytes 1597448 | tf_op jit(solution)/shard_map/ppermute | solution.py:224
  17.4 5.5 %collective-permute-start.4 = (bf16[128,2048]{1,0:T(8,128)(2,1)S(1)}, bf16[128,2048]{1,0:T(8,128)(2,1)S(1)}, u32[]{:S(2)}, u32[]{:S(2)}) collective-permute-start(bf16[128,2048]{1,0:T(8,128)(2,1)S(1)} %get-tuple-element.52), channel_id=1, source_target_pairs={{0,1},{1,0},{2,3},{3,2},{4,5},{5,4},{6,7},{7,6},{8,9},{9,8},{10,11... | collective-permute-start | bytes 1572872 | tf_op jit(solution)/shard_map/ppermute | solution.py:221
  20.8 9.3 %collective-permute-start.9 = (bf16[2080,128]{1,0:T(8,128)(2,1)S(1)}, bf16[2080,128]{1,0:T(8,128)(2,1)S(1)}, u32[]{:S(2)}, u32[]{:S(2)}) collective-permute-start(bf16[2080,128]{1,0:T(8,128)(2,1)S(1)} %collective-permute-done.5.refs_0_), channel_id=1, source_target_pairs={{0,4},{1,3},{4,8},{5,1},{8,12},{9,5},{12,14},{13,9},{14,10},{15,13... | collective-permute-start | bytes 1597448 | tf_op jit(solution)/shard_map/ppermute | solution.py:224
  23.1 12.7 %collective-permute-start.8 = (bf16[128,2048]{1,0:T(8,128)(2,1)S(1)}, bf16[128,2048]{1,0:T(8,128)(2,1)S(1)}, u32[]{:S(2)}, u32[]{:S(2)}) collective-permute-start(bf16[128,2048]{1,0:T(8,128)(2,1)S(1)} %add_convert_fusion.5), channel_id=1, source_target_pairs={{0,4},{1,3},{4,8},{5,1},{8,12},{9,5},{12,14},{13,9},{14,10},{15,13... | collective-permute-start | bytes 1572872 | tf_op jit(solution)/shard_map/ppermute | solution.py:224
  28.4 7.3 %collective-permute-start.7 = (bf16[128,2048]{1,0:T(8,128)(2,1)S(1)}, bf16[128,2048]{1,0:T(8,128)(2,1)S(1)}, u32[]{:S(2)}, u32[]{:S(2)}) collective-permute-start(bf16[128,2048]{1,0:T(8,128)(2,1)S(1)} %get-tuple-element.55), channel_id=1, source_target_pairs={{0,1},{1,0},{2,3},{3,2},{4,5},{5,4},{6,7},{7,6},{8,9},{9,8},{10,11... | collective-permute-start | bytes 1572872 | tf_op jit(solution)/shard_map/ppermute | solution.py:221
  30.1 8.2 %collective-permute-start.10 = (bf16[2080,128]{1,0:T(8,128)(2,1)S(1)}, bf16[2080,128]{1,0:T(8,128)(2,1)S(1)}, u32[]{:S(2)}, u32[]{:S(2)}) collective-permute-start(bf16[2080,128]{1,0:T(8,128)(2,1)S(1)} %collective-permute-done.9.refs_0_), channel_id=1, source_target_pairs={{0,1},{1,0},{2,3},{3,2},{4,5},{5,4},{6,7},{7,6},{8,9},{9,8},{10,11... | collective-permute-start | bytes 1597448 | tf_op jit(solution)/shard_map/ppermute | solution.py:221
  30.1 12.0 %collective-permute-start.13 = (bf16[2080,128]{1,0:T(8,128)(2,1)S(1)}, bf16[2080,128]{1,0:T(8,128)(2,1)S(1)}, u32[]{:S(2)}, u32[]{:S(2)}) collective-permute-start(bf16[2080,128]{1,0:T(8,128)(2,1)S(1)} %collective-permute-done.9.refs_0_), channel_id=1, source_target_pairs={{0,4},{1,3},{4,8},{5,1},{8,12},{9,5},{12,14},{13,9},{14,10},{15,13... | collective-permute-start | bytes 1597448 | tf_op jit(solution)/shard_map/ppermute | solution.py:224
  36.0 11.1 %collective-permute-start.12 = (bf16[128,2048]{1,0:T(8,128)(2,1)S(1)}, bf16[128,2048]{1,0:T(8,128)(2,1)S(1)}, u32[]{:S(2)}, u32[]{:S(2)}) collective-permute-start(bf16[128,2048]{1,0:T(8,128)(2,1)S(1)} %add_convert_fusion.4), channel_id=1, source_target_pairs={{0,4},{1,3},{4,8},{5,1},{8,12},{9,5},{12,14},{13,9},{14,10},{15,13... | collective-permute-start | bytes 1572872 | tf_op jit(solution)/shard_map/ppermute | solution.py:224
  42.1 7.3 %collective-permute-start.14 = (bf16[2080,128]{1,0:T(8,128)(2,1)S(1)}, bf16[2080,128]{1,0:T(8,128)(2,1)S(1)}, u32[]{:S(2)}, u32[]{:S(2)}) collective-permute-start(bf16[2080,128]{1,0:T(8,128)(2,1)S(1)} %collective-permute-done.13.refs_0_), channel_id=1, source_target_pairs={{0,1},{1,0},{2,3},{3,2},{4,5},{5,4},{6,7},{7,6},{8,9},{9,8},{10,11... | collective-permute-start | bytes 1597448 | tf_op jit(solution)/shard_map/ppermute | solution.py:221
  42.6 10.6 %collective-permute-start.17 = (bf16[2080,128]{1,0:T(8,128)(2,1)S(1)}, bf16[2080,128]{1,0:T(8,128)(2,1)S(1)}, u32[]{:S(2)}, u32[]{:S(2)}) collective-permute-start(bf16[2080,128]{1,0:T(8,128)(2,1)S(1)} %collective-permute-done.13.refs_0_), channel_id=1, source_target_pairs={{0,4},{1,3},{4,8},{5,1},{8,12},{9,5},{12,14},{13,9},{14,10},{15,13... | collective-permute-start | bytes 1597448 | tf_op jit(solution)/shard_map/ppermute | solution.py:224
  47.3 11.1 %collective-permute-start.16 = (bf16[128,2048]{1,0:T(8,128)(2,1)S(1)}, bf16[128,2048]{1,0:T(8,128)(2,1)S(1)}, u32[]{:S(2)}, u32[]{:S(2)}) collective-permute-start(bf16[128,2048]{1,0:T(8,128)(2,1)S(1)} %add_convert_fusion.3), channel_id=1, source_target_pairs={{0,4},{1,3},{4,8},{5,1},{8,12},{9,5},{12,14},{13,9},{14,10},{15,13... | collective-permute-start | bytes 1572872 | tf_op jit(solution)/shard_map/ppermute | solution.py:224
  53.2 5.2 %collective-permute-start.15 = (bf16[128,2048]{1,0:T(8,128)(2,1)S(1)}, bf16[128,2048]{1,0:T(8,128)(2,1)S(1)}, u32[]{:S(2)}, u32[]{:S(2)}) collective-permute-start(bf16[128,2048]{1,0:T(8,128)(2,1)S(1)} %get-tuple-element.63), channel_id=1, source_target_pairs={{0,1},{1,0},{2,3},{3,2},{4,5},{5,4},{6,7},{7,6},{8,9},{9,8},{10,11... | collective-permute-start | bytes 1572872 | tf_op jit(solution)/shard_map/ppermute | solution.py:221
  53.2 7.5 %collective-permute-start.18 = (bf16[2080,128]{1,0:T(8,128)(2,1)S(1)}, bf16[2080,128]{1,0:T(8,128)(2,1)S(1)}, u32[]{:S(2)}, u32[]{:S(2)}) collective-permute-start(bf16[2080,128]{1,0:T(8,128)(2,1)S(1)} %collective-permute-done.17.refs_0_), channel_id=1, source_target_pairs={{0,1},{1,0},{2,3},{3,2},{4,5},{5,4},{6,7},{7,6},{8,9},{9,8},{10,11... | collective-permute-start | bytes 1597448 | tf_op jit(solution)/shard_map/ppermute | solution.py:221
  53.7 10.8 %collective-permute-start.21 = (bf16[2080,128]{1,0:T(8,128)(2,1)S(1)}, bf16[2080,128]{1,0:T(8,128)(2,1)S(1)}, u32[]{:S(2)}, u32[]{:S(2)}) collective-permute-start(bf16[2080,128]{1,0:T(8,128)(2,1)S(1)} %collective-permute-done.17.refs_0_), channel_id=1, source_target_pairs={{0,4},{1,3},{4,8},{5,1},{8,12},{9,5},{12,14},{13,9},{14,10},{15,13... | collective-permute-start | bytes 1597448 | tf_op jit(solution)/shard_map/ppermute | solution.py:224
  58.6 11.1 %collective-permute-start.20 = (bf16[128,2048]{1,0:T(8,128)(2,1)S(1)}, bf16[128,2048]{1,0:T(8,128)(2,1)S(1)}, u32[]{:S(2)}, u32[]{:S(2)}) collective-permute-start(bf16[128,2048]{1,0:T(8,128)(2,1)S(1)} %add_convert_fusion.2), channel_id=1, source_target_pairs={{0,4},{1,3},{4,8},{5,1},{8,12},{9,5},{12,14},{13,9},{14,10},{15,13... | collective-permute-start | bytes 1572872 | tf_op jit(solution)/shard_map/ppermute | solution.py:224
  64.6 7.7 %collective-permute-start.22 = (bf16[2080,128]{1,0:T(8,128)(2,1)S(1)}, bf16[2080,128]{1,0:T(8,128)(2,1)S(1)}, u32[]{:S(2)}, u32[]{:S(2)}) collective-permute-start(bf16[2080,128]{1,0:T(8,128)(2,1)S(1)} %collective-permute-done.21.refs_0_), channel_id=1, source_target_pairs={{0,1},{1,0},{2,3},{3,2},{4,5},{5,4},{6,7},{7,6},{8,9},{9,8},{10,11... | collective-permute-start | bytes 1597448 | tf_op jit(solution)/shard_map/ppermute | solution.py:221
  65.1 11.0 %collective-permute-start.25 = (bf16[2080,128]{1,0:T(8,128)(2,1)S(1)}, bf16[2080,128]{1,0:T(8,128)(2,1)S(1)}, u32[]{:S(2)}, u32[]{:S(2)}) collective-permute-start(bf16[2080,128]{1,0:T(8,128)(2,1)S(1)} %collective-permute-done.21.refs_0_), channel_id=1, source_target_pairs={{0,4},{1,3},{4,8},{5,1},{8,12},{9,5},{12,14},{13,9},{14,10},{15,13... | collective-permute-start | bytes 1597448 | tf_op jit(solution)/shard_map/ppermute | solution.py:224
  70.0 11.1 %collective-permute-start.24 = (bf16[128,2048]{1,0:T(8,128)(2,1)S(1)}, bf16[128,2048]{1,0:T(8,128)(2,1)S(1)}, u32[]{:S(2)}, u32[]{:S(2)}) collective-permute-start(bf16[128,2048]{1,0:T(8,128)(2,1)S(1)} %add_convert_fusion.1), channel_id=1, source_target_pairs={{0,4},{1,3},{4,8},{5,1},{8,12},{9,5},{12,14},{13,9},{14,10},{15,13... | collective-permute-start | bytes 1572872 | tf_op jit(solution)/shard_map/ppermute | solution.py:224
  76.1 7.3 %collective-permute-start.26 = (bf16[2080,128]{1,0:T(8,128)(2,1)S(1)}, bf16[2080,128]{1,0:T(8,128)(2,1)S(1)}, u32[]{:S(2)}, u32[]{:S(2)}) collective-permute-start(bf16[2080,128]{1,0:T(8,128)(2,1)S(1)} %collective-permute-done.25.refs_0_), channel_id=1, source_target_pairs={{0,1},{1,0},{2,3},{3,2},{4,5},{5,4},{6,7},{7,6},{8,9},{9,8},{10,11... | collective-permute-start | bytes 1597448 | tf_op jit(solution)/shard_map/ppermute | solution.py:221
  81.3 9.2 %collective-permute-start.28 = (bf16[128,2048]{1,0:T(8,128)(2,1)S(1)}, bf16[128,2048]{1,0:T(8,128)(2,1)S(1)}, u32[]{:S(2)}, u32[]{:S(2)}) collective-permute-start(bf16[128,2048]{1,0:T(8,128)(2,1)S(1)} %add_convert_fusion), channel_id=1, source_target_pairs={{0,4},{1,3},{4,8},{5,1},{8,12},{9,5},{12,14},{13,9},{14,10},{15,13... | collective-permute-start | bytes 1572872 | tf_op jit(solution)/shard_map/ppermute | solution.py:224
  87.2 7.3 %collective-permute-start.2 = (bf16[128,2048]{1,0:T(8,128)(2,1)S(1)}, bf16[128,2048]{1,0:T(8,128)(2,1)S(1)}, u32[]{:S(2)}, u32[]{:S(2)}) collective-permute-start(bf16[128,2048]{1,0:T(8,128)(2,1)S(1)} %get-tuple-element.44), channel_id=1, source_target_pairs={{0,1},{1,0},{2,3},{3,2},{4,5},{5,4},{6,7},{7,6},{8,9},{9,8},{10,11... | collective-permute-start | bytes 1572872 | tf_op jit(solution)/shard_map/ppermute | solution.py:221
  90.6 6.4 %collective-permute-start.30 = (bf16[64,2048]{1,0:T(8,128)(2,1)S(1)}, bf16[64,2048]{1,0:T(8,128)(2,1)S(1)}, u32[]{:S(2)}, u32[]{:S(2)}) collective-permute-start(bf16[64,2048]{1,0:T(8,128)(2,1)S(1)} %shard_map.111), channel_id=1, source_target_pairs={{0,4},{1,3},{4,8},{5,1},{8,12},{9,5},{12,14},{13,9},{14,10},{15,13... | collective-permute-start | bytes 786440 | tf_op jit(solution)/shard_map/ppermute | solution.py:224
  92.8 7.0 %collective-permute-start.29 = (bf16[64,2048]{1,0:T(8,128)(2,1)S(1)}, bf16[64,2048]{1,0:T(8,128)(2,1)S(1)}, u32[]{:S(2)}, u32[]{:S(2)}) collective-permute-start(bf16[64,2048]{1,0:T(8,128)(2,1)S(1)} %shard_map.109), channel_id=1, source_target_pairs={{0,4},{1,3},{4,8},{5,1},{8,12},{9,5},{12,14},{13,9},{14,10},{15,13... | collective-permute-start | bytes 786440 | tf_op jit(solution)/shard_map/ppermute | solution.py:224
  (7 other events, 27.7 us)

commit v4 on v3

--- a/solution.py
+++ b/solution.py
@@ -252,8 +252,10 @@
             total = total + coming.astype(jnp.float32)
         total = total.astype(jnp.bfloat16)
     taken = swap(own[1])
-    halves = [add_half(own[0], taken, before, half) for half, before in enumerate(coming)]
-    return jnp.concatenate(halves).reshape(micros, held, width)
+    first = add_half(own[0], taken, coming[0], 0)
+    size = first.shape[0]
+    second = own[0][size:].astype(jnp.float32) + taken[size:].astype(jnp.float32) + coming[1].astype(jnp.float32)
+    return jnp.concatenate([first, second.astype(jnp.bfloat16)]).reshape(micros, held, width)
 
 
 def add_body(kept, taken, before, out, *, half):

time: 101 us -> 101 us (level)
  no operation moved by 1% of the time
where the time goes in v4:
time: 101 us
  Pallas kernels  34.1 us (34%)
  starting transfers between devices  33.7 us (33%)
  waiting for transfers between devices  30.5 us (30%)
  other arithmetic  2.27 us (2%)
    pallas_call x8, Pallas kernels, work(): pl.pallas_call(body, in_specs=[pl.BlockSpec(memory_space=pltpu.SMEM)] + [...  32.6 us
    ppermute x15, waiting for transfers between devices, onward(): return lax.ppermute(x, 'expert', around)  30.4 us
    ppermute x15, starting transfers between devices, onward(): return lax.ppermute(x, 'expert', around)  30 us
    ppermute x16, starting transfers between devices, swap(): return lax.ppermute(x, 'expert', across)  3.64 us
  transfers between devices with their start and end apart: 31, of which 11 were waited for; matrix products, arithmetic and copies ran while one was open for 1% of the time, Pallas kernels for 33%

profile of v4, /device:TPU:0, one launch (start us, length us, event | category | flops | bytes accessed | tf_op | source)
XLA Modules:
  0.0 100.8 jit_solution(15270696962330736817)
XLA Ops:
  1.7 2.6 %collective-permute-start = (bf16[2080,128]{1,0:T(8,128)(2,1)S(1)}, bf16[2080,128]{1,0:T(8,128)(2,1)S(1)}, u32[]{:S(2)}, u32[]{:S(2)}) collective-permute-start(bf16[2080,128]{1,0:T(8,128)(2,1)S(1)} %shard_map.100.refs_0_), channel_id=1, source_target_pairs={{0,4},{1,3},{4,8},{5,1},{8,12},{9,5},{12,14},{13,9},{14,10},{15,13... | collective-permute-start | bytes 1597448 | tf_op jit(solution)/shard_map/ppermute | solution.py:224
  4.4 6.6 %shard_map.101 = (bf16[128,2048]{1,0:T(8,128)(2,1)S(1)}, bf16[128,2048]{1,0:T(8,128)(2,1)S(1)}, bf16[2048,768]{1,0:T(8,128)(2,1)S(1)}, bf16[2048,768]{1,0:T(8,12...) custom-call(s32[1]{0:T(128)} %bitcast.2.me_ref, ...), custom_call_target="tpu_custom_call" | custom-call | flops 2717908992 | bytes 2097152 | tf_op jit(solution)/shard_map/pallas_call | solution.py:197
  13.7 3.7 %shard_map.102 = (bf16[128,2048]{1,0:T(8,128)(2,1)S(1)}, bf16[128,2048]{1,0:T(8,128)(2,1)S(1)}) custom-call(s32[1]{0:T(128)} %bitcast.2.me_ref, bf16[2080,128]{1,0:T(8,128)(2,1)S(1)} %collective-permute-done.refs_0_, bf16[2080,128]{1,0:T(8,128)(2,1)S(1)} %collective-permute-done.3.refs_1_, bf16[2048,768]{1,0:T(8,128)(2,1)S(1)} %get-tuple-element.46.refs_2_, ...), custom_call_target="tpu_custom_call" | custom-call | flops 2717908992 | bytes 2097152 | tf_op jit(solution)/shard_map/pallas_call | solution.py:197
  17.6 3.2 %collective-permute-done.5.refs_0_ = bf16[2080,128]{1,0:T(8,128)(2,1)S(1)} collective-permute-done((bf16[2080,128]{1,0:T(8,128)(2,1)S(1)}, bf16[2080,128]{1,0:T(8,128)(2,1)S(1)}, u32[]{:S(2)}, u32[]{:S(2)}) %collective-permute-start.5) | collective-permute-done | bytes 532512 | tf_op jit(solution)/shard_map/ppermute | solution.py:224
  24.7 3.7 %shard_map.103 = (bf16[128,2048]{1,0:T(8,128)(2,1)S(1)}, bf16[128,2048]{1,0:T(8,128)(2,1)S(1)}) custom-call(s32[1]{0:T(128)} %bitcast.2.me_ref, bf16[2080,128]{1,0:T(8,128)(2,1)S(1)} %collective-permute-done.5.refs_0_, bf16[2080,128]{1,0:T(8,128)(2,1)S(1)} %collective-permute-done.6.refs_1_, bf16[2048,768]{1,0:T(8,128)(2,1)S(1)} %get-tuple-element.46.refs_2_, ...), custom_call_target="tpu_custom_call" | custom-call | flops 2717908992 | bytes 2097152 | tf_op jit(solution)/shard_map/pallas_call | solution.py:197
  32.2 3.5 %collective-permute-done.8 = bf16[128,2048]{1,0:T(8,128)(2,1)S(1)} collective-permute-done((bf16[128,2048]{1,0:T(8,128)(2,1)S(1)}, bf16[128,2048]{1,0:T(8,128)(2,1)S(1)}, u32[]{:S(2)}, u32[]{:S(2)}) %collective-permute-start.8) | collective-permute-done | bytes 524320 | tf_op jit(solution)/shard_map/ppermute | solution.py:224
  36.0 2.3 %collective-permute-start.12 = (bf16[128,2048]{1,0:T(8,128)(2,1)S(1)}, bf16[128,2048]{1,0:T(8,128)(2,1)S(1)}, u32[]{:S(2)}, u32[]{:S(2)}) collective-permute-start(bf16[128,2048]{1,0:T(8,128)(2,1)S(1)} %add_convert_fusion.4), channel_id=1, source_target_pairs={{0,4},{1,3},{4,8},{5,1},{8,12},{9,5},{12,14},{13,9},{14,10},{15,13... | collective-permute-start | bytes 1572872 | tf_op jit(solution)/shard_map/ppermute | solution.py:224
  38.3 3.7 %shard_map.104 = (bf16[128,2048]{1,0:T(8,128)(2,1)S(1)}, bf16[128,2048]{1,0:T(8,128)(2,1)S(1)}) custom-call(s32[1]{0:T(128)} %bitcast.2.me_ref, bf16[2080,128]{1,0:T(8,128)(2,1)S(1)} %collective-permute-done.9.refs_0_, bf16[2080,128]{1,0:T(8,128)(2,1)S(1)} %collective-permute-done.10.refs_1_, bf16[2048,768]{1,0:T(8,128)(2,1)S(1)} %get-tuple-element.46.refs_2_, ...), custom_call_target="tpu_custom_call" | custom-call | flops 2717908992 | bytes 2097152 | tf_op jit(solution)/shard_map/pallas_call | solution.py:197
  44.2 2.9 %collective-permute-done.12 = bf16[128,2048]{1,0:T(8,128)(2,1)S(1)} collective-permute-done((bf16[128,2048]{1,0:T(8,128)(2,1)S(1)}, bf16[128,2048]{1,0:T(8,128)(2,1)S(1)}, u32[]{:S(2)}, u32[]{:S(2)}) %collective-permute-start.12) | collective-permute-done | bytes 524320 | tf_op jit(solution)/shard_map/ppermute | solution.py:224
  47.3 2.1 %collective-permute-start.16 = (bf16[128,2048]{1,0:T(8,128)(2,1)S(1)}, bf16[128,2048]{1,0:T(8,128)(2,1)S(1)}, u32[]{:S(2)}, u32[]{:S(2)}) collective-permute-start(bf16[128,2048]{1,0:T(8,128)(2,1)S(1)} %add_convert_fusion.3), channel_id=1, source_target_pairs={{0,4},{1,3},{4,8},{5,1},{8,12},{9,5},{12,14},{13,9},{14,10},{15,13... | collective-permute-start | bytes 1572872 | tf_op jit(solution)/shard_map/ppermute | solution.py:224
  49.4 3.7 %shard_map.105 = (bf16[128,2048]{1,0:T(8,128)(2,1)S(1)}, bf16[128,2048]{1,0:T(8,128)(2,1)S(1)}) custom-call(s32[1]{0:T(128)} %bitcast.2.me_ref, bf16[2080,128]{1,0:T(8,128)(2,1)S(1)} %collective-permute-done.13.refs_0_, bf16[2080,128]{1,0:T(8,128)(2,1)S(1)} %collective-permute-done.14.refs_1_, bf16[2048,768]{1,0:T(8,128)(2,1)S(1)} %get-tuple-element.46.refs_2_, ...), custom_call_target="tpu_custom_call" | custom-call | flops 2717908992 | bytes 2097152 | tf_op jit(solution)/shard_map/pallas_call | solution.py:197
  55.3 3.1 %collective-permute-done.16 = bf16[128,2048]{1,0:T(8,128)(2,1)S(1)} collective-permute-done((bf16[128,2048]{1,0:T(8,128)(2,1)S(1)}, bf16[128,2048]{1,0:T(8,128)(2,1)S(1)}, u32[]{:S(2)}, u32[]{:S(2)}) %collective-permute-start.16) | collective-permute-done | bytes 524320 | tf_op jit(solution)/shard_map/ppermute | solution.py:224
  58.6 2.1 %collective-permute-start.20 = (bf16[128,2048]{1,0:T(8,128)(2,1)S(1)}, bf16[128,2048]{1,0:T(8,128)(2,1)S(1)}, u32[]{:S(2)}, u32[]{:S(2)}) collective-permute-start(bf16[128,2048]{1,0:T(8,128)(2,1)S(1)} %add_convert_fusion.2), channel_id=1, source_target_pairs={{0,4},{1,3},{4,8},{5,1},{8,12},{9,5},{12,14},{13,9},{14,10},{15,13... | collective-permute-start | bytes 1572872 | tf_op jit(solution)/shard_map/ppermute | solution.py:224
  60.8 3.7 %shard_map.106 = (bf16[128,2048]{1,0:T(8,128)(2,1)S(1)}, bf16[128,2048]{1,0:T(8,128)(2,1)S(1)}) custom-call(s32[1]{0:T(128)} %bitcast.2.me_ref, bf16[2080,128]{1,0:T(8,128)(2,1)S(1)} %collective-permute-done.17.refs_0_, bf16[2080,128]{1,0:T(8,128)(2,1)S(1)} %collective-permute-done.18.refs_1_, bf16[2048,768]{1,0:T(8,128)(2,1)S(1)} %get-tuple-element.46.refs_2_, ...), custom_call_target="tpu_custom_call" | custom-call | flops 2717908992 | bytes 2097152 | tf_op jit(solution)/shard_map/pallas_call | solution.py:197
  66.6 3.1 %collective-permute-done.20 = bf16[128,2048]{1,0:T(8,128)(2,1)S(1)} collective-permute-done((bf16[128,2048]{1,0:T(8,128)(2,1)S(1)}, bf16[128,2048]{1,0:T(8,128)(2,1)S(1)}, u32[]{:S(2)}, u32[]{:S(2)}) %collective-permute-start.20) | collective-permute-done | bytes 524320 | tf_op jit(solution)/shard_map/ppermute | solution.py:224
  70.0 2.3 %collective-permute-start.24 = (bf16[128,2048]{1,0:T(8,128)(2,1)S(1)}, bf16[128,2048]{1,0:T(8,128)(2,1)S(1)}, u32[]{:S(2)}, u32[]{:S(2)}) collective-permute-start(bf16[128,2048]{1,0:T(8,128)(2,1)S(1)} %add_convert_fusion.1), channel_id=1, source_target_pairs={{0,4},{1,3},{4,8},{5,1},{8,12},{9,5},{12,14},{13,9},{14,10},{15,13... | collective-permute-start | bytes 1572872 | tf_op jit(solution)/shard_map/ppermute | solution.py:224
  72.3 3.7 %shard_map.107 = (bf16[128,2048]{1,0:T(8,128)(2,1)S(1)}, bf16[128,2048]{1,0:T(8,128)(2,1)S(1)}) custom-call(s32[1]{0:T(128)} %bitcast.2.me_ref, bf16[2080,128]{1,0:T(8,128)(2,1)S(1)} %collective-permute-done.21.refs_0_, bf16[2080,128]{1,0:T(8,128)(2,1)S(1)} %collective-permute-done.22.refs_1_, bf16[2048,768]{1,0:T(8,128)(2,1)S(1)} %get-tuple-element.46.refs_2_, ...), custom_call_target="tpu_custom_call" | custom-call | flops 2717908992 | bytes 2097152 | tf_op jit(solution)/shard_map/pallas_call | solution.py:197
  76.6 4.4 %collective-permute-done.24 = bf16[128,2048]{1,0:T(8,128)(2,1)S(1)} collective-permute-done((bf16[128,2048]{1,0:T(8,128)(2,1)S(1)}, bf16[128,2048]{1,0:T(8,128)(2,1)S(1)}, u32[]{:S(2)}, u32[]{:S(2)}) %collective-permute-start.24) | collective-permute-done | bytes 524320 | tf_op jit(solution)/shard_map/ppermute | solution.py:224
  81.3 2.1 %collective-permute-start.28 = (bf16[128,2048]{1,0:T(8,128)(2,1)S(1)}, bf16[128,2048]{1,0:T(8,128)(2,1)S(1)}, u32[]{:S(2)}, u32[]{:S(2)}) collective-permute-start(bf16[128,2048]{1,0:T(8,128)(2,1)S(1)} %add_convert_fusion), channel_id=1, source_target_pairs={{0,4},{1,3},{4,8},{5,1},{8,12},{9,5},{12,14},{13,9},{14,10},{15,13... | collective-permute-start | bytes 1572872 | tf_op jit(solution)/shard_map/ppermute | solution.py:224
  83.4 3.7 %shard_map.108 = (bf16[128,2048]{1,0:T(8,128)(2,1)S(1)}, bf16[128,2048]{1,0:T(8,128)(2,1)S(1)}) custom-call(s32[1]{0:T(128)} %bitcast.2.me_ref, bf16[2080,128]{1,0:T(8,128)(2,1)S(1)} %collective-permute-done.25.refs_0_, bf16[2080,128]{1,0:T(8,128)(2,1)S(1)} %collective-permute-done.26.refs_1_, bf16[2048,768]{1,0:T(8,128)(2,1)S(1)} %get-tuple-element.46.refs_2_, ...), custom_call_target="tpu_custom_call" | custom-call | flops 2717908992 | bytes 2097152 | tf_op jit(solution)/shard_map/pallas_call | solution.py:197
  87.7 2.8 %collective-permute-done.28.before = bf16[128,2048]{1,0:T(8,128)(2,1)S(1)} collective-permute-done((bf16[128,2048]{1,0:T(8,128)(2,1)S(1)}, bf16[128,2048]{1,0:T(8,128)(2,1)S(1)}, u32[]{:S(2)}, u32[]{:S(2)}) %collective-permute-start.28) | collective-permute-done | bytes 524320 | tf_op jit(solution)/shard_map/ppermute | solution.py:224
  90.6 2.1 %collective-permute-start.30 = (bf16[64,2048]{1,0:T(8,128)(2,1)S(1)}, bf16[64,2048]{1,0:T(8,128)(2,1)S(1)}, u32[]{:S(2)}, u32[]{:S(2)}) collective-permute-start(bf16[64,2048]{1,0:T(8,128)(2,1)S(1)} %shard_map.111), channel_id=1, source_target_pairs={{0,4},{1,3},{4,8},{5,1},{8,12},{9,5},{12,14},{13,9},{14,10},{15,13... | collective-permute-start | bytes 786440 | tf_op jit(solution)/shard_map/ppermute | solution.py:224
  94.5 2.6 %collective-permute-done.30 = bf16[64,2048]{1,0:T(8,128)(2,1)S(1)} collective-permute-done((bf16[64,2048]{1,0:T(8,128)(2,1)S(1)}, bf16[64,2048]{1,0:T(8,128)(2,1)S(1)}, u32[]{:S(2)}, u32[]{:S(2)}) %collective-permute-start.30) | collective-permute-done | bytes 262176 | tf_op jit(solution)/shard_map/ppermute | solution.py:224
  97.1 2.7 %collective-permute-done.29.before = bf16[64,2048]{1,0:T(8,128)(2,1)S(1)} collective-permute-done((bf16[64,2048]{1,0:T(8,128)(2,1)S(1)}, bf16[64,2048]{1,0:T(8,128)(2,1)S(1)}, u32[]{:S(2)}, u32[]{:S(2)}) %collective-permute-start.29) | collective-permute-done | bytes 262176 | tf_op jit(solution)/shard_map/ppermute | solution.py:224
  (58 shorter events, 23.9 us)
Async XLA Ops:
  1.7 9.8 %collective-permute-start = (bf16[2080,128]{1,0:T(8,128)(2,1)S(1)}, bf16[2080,128]{1,0:T(8,128)(2,1)S(1)}, u32[]{:S(2)}, u32[]{:S(2)}) collective-permute-start(bf16[2080,128]{1,0:T(8,128)(2,1)S(1)} %shard_map.100.refs_0_), channel_id=1, source_target_pairs={{0,4},{1,3},{4,8},{5,1},{8,12},{9,5},{12,14},{13,9},{14,10},{15,13... | collective-permute-start | bytes 1597448 | tf_op jit(solution)/shard_map/ppermute | solution.py:224
  11.6 9.3 %collective-permute-start.5 = (bf16[2080,128]{1,0:T(8,128)(2,1)S(1)}, bf16[2080,128]{1,0:T(8,128)(2,1)S(1)}, u32[]{:S(2)}, u32[]{:S(2)}) collective-permute-start(bf16[2080,128]{1,0:T(8,128)(2,1)S(1)} %collective-permute-done.refs_0_), channel_id=1, source_target_pairs={{0,4},{1,3},{4,8},{5,1},{8,12},{9,5},{12,14},{13,9},{14,10},{15,13... | collective-permute-start | bytes 1597448 | tf_op jit(solution)/shard_map/ppermute | solution.py:224
  17.4 5.5 %collective-permute-start.4 = (bf16[128,2048]{1,0:T(8,128)(2,1)S(1)}, bf16[128,2048]{1,0:T(8,128)(2,1)S(1)}, u32[]{:S(2)}, u32[]{:S(2)}) collective-permute-start(bf16[128,2048]{1,0:T(8,128)(2,1)S(1)} %get-tuple-element.52), channel_id=1, source_target_pairs={{0,1},{1,0},{2,3},{3,2},{4,5},{5,4},{6,7},{7,6},{8,9},{9,8},{10,11... | collective-permute-start | bytes 1572872 | tf_op jit(solution)/shard_map/ppermute | solution.py:221
  20.8 9.3 %collective-permute-start.9 = (bf16[2080,128]{1,0:T(8,128)(2,1)S(1)}, bf16[2080,128]{1,0:T(8,128)(2,1)S(1)}, u32[]{:S(2)}, u32[]{:S(2)}) collective-permute-start(bf16[2080,128]{1,0:T(8,128)(2,1)S(1)} %collective-permute-done.5.refs_0_), channel_id=1, source_target_pairs={{0,4},{1,3},{4,8},{5,1},{8,12},{9,5},{12,14},{13,9},{14,10},{15,13... | collective-permute-start | bytes 1597448 | tf_op jit(solution)/shard_map/ppermute | solution.py:224
  23.1 12.7 %collective-permute-start.8 = (bf16[128,2048]{1,0:T(8,128)(2,1)S(1)}, bf16[128,2048]{1,0:T(8,128)(2,1)S(1)}, u32[]{:S(2)}, u32[]{:S(2)}) collective-permute-start(bf16[128,2048]{1,0:T(8,128)(2,1)S(1)} %add_convert_fusion.5), channel_id=1, source_target_pairs={{0,4},{1,3},{4,8},{5,1},{8,12},{9,5},{12,14},{13,9},{14,10},{15,13... | collective-permute-start | bytes 1572872 | tf_op jit(solution)/shard_map/ppermute | solution.py:224
  28.4 7.3 %collective-permute-start.7 = (bf16[128,2048]{1,0:T(8,128)(2,1)S(1)}, bf16[128,2048]{1,0:T(8,128)(2,1)S(1)}, u32[]{:S(2)}, u32[]{:S(2)}) collective-permute-start(bf16[128,2048]{1,0:T(8,128)(2,1)S(1)} %get-tuple-element.55), channel_id=1, source_target_pairs={{0,1},{1,0},{2,3},{3,2},{4,5},{5,4},{6,7},{7,6},{8,9},{9,8},{10,11... | collective-permute-start | bytes 1572872 | tf_op jit(solution)/shard_map/ppermute | solution.py:221
  30.1 8.2 %collective-permute-start.10 = (bf16[2080,128]{1,0:T(8,128)(2,1)S(1)}, bf16[2080,128]{1,0:T(8,128)(2,1)S(1)}, u32[]{:S(2)}, u32[]{:S(2)}) collective-permute-start(bf16[2080,128]{1,0:T(8,128)(2,1)S(1)} %collective-permute-done.9.refs_0_), channel_id=1, source_target_pairs={{0,1},{1,0},{2,3},{3,2},{4,5},{5,4},{6,7},{7,6},{8,9},{9,8},{10,11... | collective-permute-start | bytes 1597448 | tf_op jit(solution)/shard_map/ppermute | solution.py:221
  30.1 12.0 %collective-permute-start.13 = (bf16[2080,128]{1,0:T(8,128)(2,1)S(1)}, bf16[2080,128]{1,0:T(8,128)(2,1)S(1)}, u32[]{:S(2)}, u32[]{:S(2)}) collective-permute-start(bf16[2080,128]{1,0:T(8,128)(2,1)S(1)} %collective-permute-done.9.refs_0_), channel_id=1, source_target_pairs={{0,4},{1,3},{4,8},{5,1},{8,12},{9,5},{12,14},{13,9},{14,10},{15,13... | collective-permute-start | bytes 1597448 | tf_op jit(solution)/shard_map/ppermute | solution.py:224
  36.0 11.1 %collective-permute-start.12 = (bf16[128,2048]{1,0:T(8,128)(2,1)S(1)}, bf16[128,2048]{1,0:T(8,128)(2,1)S(1)}, u32[]{:S(2)}, u32[]{:S(2)}) collective-permute-start(bf16[128,2048]{1,0:T(8,128)(2,1)S(1)} %add_convert_fusion.4), channel_id=1, source_target_pairs={{0,4},{1,3},{4,8},{5,1},{8,12},{9,5},{12,14},{13,9},{14,10},{15,13... | collective-permute-start | bytes 1572872 | tf_op jit(solution)/shard_map/ppermute | solution.py:224
  42.1 7.3 %collective-permute-start.14 = (bf16[2080,128]{1,0:T(8,128)(2,1)S(1)}, bf16[2080,128]{1,0:T(8,128)(2,1)S(1)}, u32[]{:S(2)}, u32[]{:S(2)}) collective-permute-start(bf16[2080,128]{1,0:T(8,128)(2,1)S(1)} %collective-permute-done.13.refs_0_), channel_id=1, source_target_pairs={{0,1},{1,0},{2,3},{3,2},{4,5},{5,4},{6,7},{7,6},{8,9},{9,8},{10,11... | collective-permute-start | bytes 1597448 | tf_op jit(solution)/shard_map/ppermute | solution.py:221
  42.6 10.6 %collective-permute-start.17 = (bf16[2080,128]{1,0:T(8,128)(2,1)S(1)}, bf16[2080,128]{1,0:T(8,128)(2,1)S(1)}, u32[]{:S(2)}, u32[]{:S(2)}) collective-permute-start(bf16[2080,128]{1,0:T(8,128)(2,1)S(1)} %collective-permute-done.13.refs_0_), channel_id=1, source_target_pairs={{0,4},{1,3},{4,8},{5,1},{8,12},{9,5},{12,14},{13,9},{14,10},{15,13... | collective-permute-start | bytes 1597448 | tf_op jit(solution)/shard_map/ppermute | solution.py:224
  47.3 11.1 %collective-permute-start.16 = (bf16[128,2048]{1,0:T(8,128)(2,1)S(1)}, bf16[128,2048]{1,0:T(8,128)(2,1)S(1)}, u32[]{:S(2)}, u32[]{:S(2)}) collective-permute-start(bf16[128,2048]{1,0:T(8,128)(2,1)S(1)} %add_convert_fusion.3), channel_id=1, source_target_pairs={{0,4},{1,3},{4,8},{5,1},{8,12},{9,5},{12,14},{13,9},{14,10},{15,13... | collective-permute-start | bytes 1572872 | tf_op jit(solution)/shard_map/ppermute | solution.py:224
  53.2 5.2 %collective-permute-start.15 = (bf16[128,2048]{1,0:T(8,128)(2,1)S(1)}, bf16[128,2048]{1,0:T(8,128)(2,1)S(1)}, u32[]{:S(2)}, u32[]{:S(2)}) collective-permute-start(bf16[128,2048]{1,0:T(8,128)(2,1)S(1)} %get-tuple-element.63), channel_id=1, source_target_pairs={{0,1},{1,0},{2,3},{3,2},{4,5},{5,4},{6,7},{7,6},{8,9},{9,8},{10,11... | collective-permute-start | bytes 1572872 | tf_op jit(solution)/shard_map/ppermute | solution.py:221
  53.2 7.5 %collective-permute-start.18 = (bf16[2080,128]{1,0:T(8,128)(2,1)S(1)}, bf16[2080,128]{1,0:T(8,128)(2,1)S(1)}, u32[]{:S(2)}, u32[]{:S(2)}) collective-permute-start(bf16[2080,128]{1,0:T(8,128)(2,1)S(1)} %collective-permute-done.17.refs_0_), channel_id=1, source_target_pairs={{0,1},{1,0},{2,3},{3,2},{4,5},{5,4},{6,7},{7,6},{8,9},{9,8},{10,11... | collective-permute-start | bytes 1597448 | tf_op jit(solution)/shard_map/ppermute | solution.py:221
  53.7 10.8 %collective-permute-start.21 = (bf16[2080,128]{1,0:T(8,128)(2,1)S(1)}, bf16[2080,128]{1,0:T(8,128)(2,1)S(1)}, u32[]{:S(2)}, u32[]{:S(2)}) collective-permute-start(bf16[2080,128]{1,0:T(8,128)(2,1)S(1)} %collective-permute-done.17.refs_0_), channel_id=1, source_target_pairs={{0,4},{1,3},{4,8},{5,1},{8,12},{9,5},{12,14},{13,9},{14,10},{15,13... | collective-permute-start | bytes 1597448 | tf_op jit(solution)/shard_map/ppermute | solution.py:224
  58.6 11.1 %collective-permute-start.20 = (bf16[128,2048]{1,0:T(8,128)(2,1)S(1)}, bf16[128,2048]{1,0:T(8,128)(2,1)S(1)}, u32[]{:S(2)}, u32[]{:S(2)}) collective-permute-start(bf16[128,2048]{1,0:T(8,128)(2,1)S(1)} %add_convert_fusion.2), channel_id=1, source_target_pairs={{0,4},{1,3},{4,8},{5,1},{8,12},{9,5},{12,14},{13,9},{14,10},{15,13... | collective-permute-start | bytes 1572872 | tf_op jit(solution)/shard_map/ppermute | solution.py:224
  64.6 7.7 %collective-permute-start.22 = (bf16[2080,128]{1,0:T(8,128)(2,1)S(1)}, bf16[2080,128]{1,0:T(8,128)(2,1)S(1)}, u32[]{:S(2)}, u32[]{:S(2)}) collective-permute-start(bf16[2080,128]{1,0:T(8,128)(2,1)S(1)} %collective-permute-done.21.refs_0_), channel_id=1, source_target_pairs={{0,1},{1,0},{2,3},{3,2},{4,5},{5,4},{6,7},{7,6},{8,9},{9,8},{10,11... | collective-permute-start | bytes 1597448 | tf_op jit(solution)/shard_map/ppermute | solution.py:221
  65.1 11.0 %collective-permute-start.25 = (bf16[2080,128]{1,0:T(8,128)(2,1)S(1)}, bf16[2080,128]{1,0:T(8,128)(2,1)S(1)}, u32[]{:S(2)}, u32[]{:S(2)}) collective-permute-start(bf16[2080,128]{1,0:T(8,128)(2,1)S(1)} %collective-permute-done.21.refs_0_), channel_id=1, source_target_pairs={{0,4},{1,3},{4,8},{5,1},{8,12},{9,5},{12,14},{13,9},{14,10},{15,13... | collective-permute-start | bytes 1597448 | tf_op jit(solution)/shard_map/ppermute | solution.py:224
  70.0 11.1 %collective-permute-start.24 = (bf16[128,2048]{1,0:T(8,128)(2,1)S(1)}, bf16[128,2048]{1,0:T(8,128)(2,1)S(1)}, u32[]{:S(2)}, u32[]{:S(2)}) collective-permute-start(bf16[128,2048]{1,0:T(8,128)(2,1)S(1)} %add_convert_fusion.1), channel_id=1, source_target_pairs={{0,4},{1,3},{4,8},{5,1},{8,12},{9,5},{12,14},{13,9},{14,10},{15,13... | collective-permute-start | bytes 1572872 | tf_op jit(solution)/shard_map/ppermute | solution.py:224
  76.1 7.3 %collective-permute-start.26 = (bf16[2080,128]{1,0:T(8,128)(2,1)S(1)}, bf16[2080,128]{1,0:T(8,128)(2,1)S(1)}, u32[]{:S(2)}, u32[]{:S(2)}) collective-permute-start(bf16[2080,128]{1,0:T(8,128)(2,1)S(1)} %collective-permute-done.25.refs_0_), channel_id=1, source_target_pairs={{0,1},{1,0},{2,3},{3,2},{4,5},{5,4},{6,7},{7,6},{8,9},{9,8},{10,11... | collective-permute-start | bytes 1597448 | tf_op jit(solution)/shard_map/ppermute | solution.py:221
  81.3 9.2 %collective-permute-start.28 = (bf16[128,2048]{1,0:T(8,128)(2,1)S(1)}, bf16[128,2048]{1,0:T(8,128)(2,1)S(1)}, u32[]{:S(2)}, u32[]{:S(2)}) collective-permute-start(bf16[128,2048]{1,0:T(8,128)(2,1)S(1)} %add_convert_fusion), channel_id=1, source_target_pairs={{0,4},{1,3},{4,8},{5,1},{8,12},{9,5},{12,14},{13,9},{14,10},{15,13... | collective-permute-start | bytes 1572872 | tf_op jit(solution)/shard_map/ppermute | solution.py:224
  87.2 7.3 %collective-permute-start.2 = (bf16[128,2048]{1,0:T(8,128)(2,1)S(1)}, bf16[128,2048]{1,0:T(8,128)(2,1)S(1)}, u32[]{:S(2)}, u32[]{:S(2)}) collective-permute-start(bf16[128,2048]{1,0:T(8,128)(2,1)S(1)} %get-tuple-element.44), channel_id=1, source_target_pairs={{0,1},{1,0},{2,3},{3,2},{4,5},{5,4},{6,7},{7,6},{8,9},{9,8},{10,11... | collective-permute-start | bytes 1572872 | tf_op jit(solution)/shard_map/ppermute | solution.py:221
  90.6 6.4 %collective-permute-start.30 = (bf16[64,2048]{1,0:T(8,128)(2,1)S(1)}, bf16[64,2048]{1,0:T(8,128)(2,1)S(1)}, u32[]{:S(2)}, u32[]{:S(2)}) collective-permute-start(bf16[64,2048]{1,0:T(8,128)(2,1)S(1)} %shard_map.111), channel_id=1, source_target_pairs={{0,4},{1,3},{4,8},{5,1},{8,12},{9,5},{12,14},{13,9},{14,10},{15,13... | collective-permute-start | bytes 786440 | tf_op jit(solution)/shard_map/ppermute | solution.py:224
  92.8 7.0 %collective-permute-start.29 = (bf16[64,2048]{1,0:T(8,128)(2,1)S(1)}, bf16[64,2048]{1,0:T(8,128)(2,1)S(1)}, u32[]{:S(2)}, u32[]{:S(2)}) collective-permute-start(bf16[64,2048]{1,0:T(8,128)(2,1)S(1)} %shard_map.109), channel_id=1, source_target_pairs={{0,4},{1,3},{4,8},{5,1},{8,12},{9,5},{12,14},{13,9},{14,10},{15,13... | collective-permute-start | bytes 786440 | tf_op jit(solution)/shard_map/ppermute | solution.py:224
  (7 other events, 27.7 us)
